TPU v7x, 512 devices: a whole 4x4x16 slice. The times are simulated.
512 devices in a mesh: pipe: 16 (over z), expert: 32 (over x, y, core).
Axes of the slice: x: 4, y: 4, z: 16, core: 2. Of those that a mesh axis runs over, the one named last changes fastest.
Arguments:
- forward_in: bfloat16 [16, 256, 3584], P('pipe', 'expert'), may hold values from -6 to 6
- forward_new: bfloat16 [1, 256, 3584], P(None, 'expert'), may hold values from -6 to 6
- grad_in: bfloat16 [16, 256, 3584], P('pipe', 'expert'), may hold values from -6 to 6
- grad_new: bfloat16 [1, 256, 3584], P(None, 'expert'), may hold values from -6 to 6
- saved_inputs: bfloat16 [2, 16, 256, 3584], P(None, 'pipe', 'expert'), may hold values from -6 to 6
- forward_ids: int32 [2, 16, 256, 2], P(None, 'pipe', 'expert'), may hold values from 0 to 3, all different within a row; in each aligned block of 8 rows (0 to 7, 8 to 15, ..., all dimensions but the last counted through in order) at most 6 rows name the same one
- backward_ids: int32 [2, 16, 256, 2], P(None, 'pipe', 'expert'), may hold values from 0 to 3, all different within a row; in each aligned block of 8 rows (0 to 7, 8 to 15, ..., all dimensions but the last counted through in order) at most 6 rows name the same one
- norm_gain: bfloat16 [16, 3584], P('pipe'), may hold values from 0.5 to 1.5
- router: bfloat16 [16, 3584, 4], P('pipe'), may hold values from -0.09375 to 0.09375
- gate_proj: bfloat16 [16, 3584, 4096], P('pipe', None, 'expert'), may hold values from -0.09375 to 0.09375
- up_proj: bfloat16 [16, 3584, 4096], P('pipe', None, 'expert'), may hold values from -0.09375 to 0.09375
- down_proj: bfloat16 [16, 4096, 3584], P('pipe', 'expert'), may hold values from -0.1875 to 0.1875
Outputs:
- forward_out: bfloat16 [2, 16, 256, 3584], P(None, 'pipe', 'expert')
- input_grads: bfloat16 [2, 16, 256, 3584], P(None, 'pipe', 'expert')
Inputs may be any that keep to these rules, and one draw needn't show every extreme that they name: `forward_ids`: each token names 2 different experts. Within the 8 rows of one device (aligned blocks along all leading dimensions) no expert is named more than 6 times, and in every draw some block names some expert exactly 6 times. `backward_ids`: as for forward_ids.
All inputs are finite; a program needn't handle non-finite values.
Results may differ from a plain program's by a relative error of at most 0.02.
Values may be sent and summed in bfloat16 or wider, within the bound.
No kernel may reach another device: no remote copies, remote signals or barrier semaphores. Data moves between devices by JAX's collectives and lax.ppermute only.
A program may use at most 128 MiB of HBM per device.

v0:
```python
import functools

import jax
import jax.numpy as jnp
import numpy as np
from jax import lax
from jax.experimental import pallas as pl
from jax.experimental.pallas import tpu as pltpu
from jax.sharding import Mesh
from jax.sharding import PartitionSpec as P

CAP = 6
EXPERTS = 4
TOK = 8
CHIPS = 16
UNITS = 4
BLOCK = UNITS * CAP
ROWS = CHIPS * BLOCK
PACK = 128

routed_scale = 2.5
norm_eps = 1e-06
f32 = jnp.float32
bf16 = jnp.bfloat16

NT = (((1,), (1,)), ((), ()))


def dot(a, b):
    return jnp.dot(a, b, preferred_element_type=f32)


def dot_nt(a, b):
    return lax.dot_general(a, b, NT, preferred_element_type=f32)


def iota(shape, axis):
    return lax.broadcasted_iota(jnp.int32, shape, axis)


def whole(index, size):
    return jnp.floor((index.astype(f32) + 0.5) * (1.0 / size))


def row_codes(shape, axis):
    row = iota(shape, axis)
    expert = whole(row, ROWS // EXPERTS)
    offset = row.astype(f32) - BLOCK * whole(row, BLOCK)
    unit = jnp.floor((offset + 0.5) * (1.0 / CAP))
    return expert, unit, offset - CAP * unit


def tables(ids):
    cols = jnp.concatenate([u.astype(f32) for u in ids], 0)
    n = cols.shape[0]
    i, j = iota((n, n), 0), iota((n, n), 1)
    same = whole(i, TOK) == whole(j, TOK)
    col = [cols[:, k : k + 1] for k in range(2)]
    lane = [jnp.sum(jnp.where(i == j, c, 0.0), 0, keepdims=True) for c in col]
    col_pos, lane_pos = [], []
    for k in range(2):
        ahead = same & (j < i) & ((lane[0] == col[k]) | (lane[1] == col[k]))
        col_pos.append(jnp.sum(jnp.where(ahead, 1.0, 0.0), 1, keepdims=True))
        ahead = same & (i < j) & ((col[0] == lane[k]) | (col[1] == lane[k]))
        lane_pos.append(jnp.sum(jnp.where(ahead, 1.0, 0.0), 0, keepdims=True))
    return col, col_pos, lane, lane_pos


def dispatch(rows, ids):
    _, _, lane, lane_pos = tables(ids)
    shape = (ROWS, UNITS * TOK)
    expert, unit, slot = row_codes(shape, 0)
    hit = (expert == lane[0]) & (slot == lane_pos[0]) | (expert == lane[1]) & (slot == lane_pos[1])
    hit = hit & (unit == whole(iota(shape, 1), TOK))
    table = jnp.where(hit, 1.0, 0.0).astype(bf16)
    stacked = jnp.concatenate(rows, 0).astype(bf16)
    return dot(table, stacked).astype(bf16)


def norm_rows(wide, gain):
    inverse = lax.rsqrt(jnp.mean(wide * wide, -1, keepdims=True) + norm_eps)
    return inverse, (wide * inverse * gain).astype(bf16).astype(f32)


def route(normed, inverse, ids, router):
    logits = dot(normed.astype(bf16), router)
    lanes = iota(logits.shape, 1)
    affin = [
        jax.nn.sigmoid(jnp.sum(jnp.where(lanes == ids[:, k : k + 1], logits, 0.0), -1, keepdims=True))
        for k in range(2)
    ]
    at = iota((TOK, 128), 1)
    return jnp.where(at == 0, affin[0], jnp.where(at == 1, affin[1], inverse))


def prepare_kernel(x_ref, s_ref, c_ref, gain_ref, router_ref, fid_ref, bid_ref, out_ref, stat_ref):
    gain = gain_ref[...].astype(f32)
    router = router_ref[0]
    ids = [fid_ref[0, 0], bid_ref[0, 0], bid_ref[1, 0]]
    rows = []
    for n, wide in enumerate((x_ref[0], s_ref[0, 0], s_ref[1, 0])):
        inverse, normed = norm_rows(wide.astype(f32), gain)
        stat_ref[n] = route(normed, inverse, ids[n], router)
        rows.append(normed)
    units = [rows[0], rows[1], c_ref[0].astype(f32), rows[2]]
    out_ref[...] = dispatch(units, [ids[0], ids[1], ids[1], ids[2]])


def again_kernel(
    sec_ref, y_ref, fnew_ref, b_ref, gnew_ref, gain_ref, router_ref, fid_ref, bid_ref,
    out_ref, x_ref, c_ref, stat_ref, *, last,
):
    first = sec_ref[0, 0] == 0
    final = sec_ref[0, 0] == last
    x = jnp.where(first, fnew_ref[0].astype(f32), y_ref[...].astype(f32))
    c = jnp.where(final, gnew_ref[0].astype(f32), b_ref[...].astype(f32))
    x_ref[...] = x.astype(bf16)
    c_ref[...] = c.astype(bf16)
    ids = [fid_ref[1, 0], bid_ref[1, 0]]
    inverse, normed = norm_rows(x, gain_ref[...].astype(f32))
    stat_ref[...] = route(normed, inverse, ids[0], router_ref[0])
    half = x.shape[1] // 2
    units = [normed[:, :half], c[:, :half], normed[:, half:], c[:, half:]]
    out_ref[...] = dispatch(units, ids + ids)


def roll_up(value, count):
    return pltpu.roll(value, value.shape[0] - count, 0)


def experts(pre, grad_act, gu_ref, down_ref, out_ref):
    hidden = grad_act.shape[1]
    offset = iota((CHIPS, BLOCK, hidden), 1).reshape(ROWS, hidden)
    forward = offset < CAP
    backward = (offset >= CAP) & (offset < 2 * CAP)
    pre_gate, pre_up = pre[:, :hidden], pre[:, hidden:]
    sigma = jax.nn.sigmoid(pre_gate)
    silu = pre_gate * sigma
    active = silu * pre_up
    dg = jnp.sum(jnp.where(backward, active.astype(bf16).astype(f32) * grad_act, 0.0), 1, keepdims=True)
    grad_up = grad_act * silu
    grad_gate = grad_act * pre_up * sigma * (1.0 + pre_gate * (1.0 - sigma))
    parts = [
        jnp.where(forward, active, 0.0),
        jnp.where(backward, grad_gate, 0.0),
        jnp.where(backward, grad_up, 0.0),
    ]
    parts = [(p + pltpu.roll(p, 2 * CAP, 0)).astype(bf16) for p in parts]
    grads = jnp.concatenate(parts[1:], 1)
    width = down_ref.shape[1] // 2
    step = 256
    left = iota((CHIPS, BLOCK, step), 1).reshape(ROWS, step) < 2 * CAP
    for n in range(0, width, step):
        sides = []
        for at in (n, n + width):
            side = dot(parts[0], down_ref[:, at : at + step])
            sides.append(side + dot_nt(grads, gu_ref[at : at + step, :]))
        out_ref[:, n : n + step] = jnp.where(left, sides[0], sides[1]).astype(bf16)
    high = dg.astype(bf16).astype(f32)
    low = pltpu.roll(jnp.broadcast_to(dg - high, (ROWS, PACK)), 2 * CAP, 0)
    high = jnp.broadcast_to(high, (ROWS, PACK))
    out_ref[:, width : width + PACK] = jnp.where(left[:, :PACK], high, low).astype(bf16)


def experts_first_kernel(in_ref, gu_ref, down_ref, out_ref, keep_ref):
    pre = dot(in_ref[...], gu_ref[...])
    grad_act = roll_up(dot_nt(in_ref[...], down_ref[...]), CAP)
    keep_ref[...] = roll_up(pre, 2 * CAP)
    experts(pre, grad_act, gu_ref, down_ref, out_ref)


def experts_second_kernel(in_ref, keep_ref, gu_ref, down_ref, out_ref):
    width = in_ref.shape[1]
    rows = in_ref[...]
    pre = dot(rows, gu_ref[:width, :]) + roll_up(dot(rows, gu_ref[width:, :]), 2 * CAP)
    grad_act = dot_nt(rows, down_ref[:, :width]) + roll_up(dot_nt(rows, down_ref[:, width:]), 2 * CAP)
    offset = iota((CHIPS, BLOCK, pre.shape[1]), 1).reshape(pre.shape)
    pre = jnp.where(offset < CAP, pre, keep_ref[...])
    experts(pre, grad_act, gu_ref, down_ref, out_ref)


def combine(in_ref, x, s, cot, x_stat, s_stat, fid, bid, gain, router_rows):
    col, col_pos, _, _ = tables([fid, bid])
    shape = (TOK, ROWS)
    expert, unit, slot = row_codes(shape, 1)
    blocks = []
    for h in range(2):
        for u in range(2):
            at = slice(u * TOK, (u + 1) * TOK)
            for k in range(2):
                hit = (expert == col[k][at]) & (slot == col_pos[k][at]) & (unit == 2 * h + u)
                blocks.append(jnp.where(hit, 1.0, 0.0))
    table = jnp.concatenate(blocks, 0).astype(bf16)
    picked = dot(table, in_ref[...])
    width = x.shape[1] // 2

    def taken(u, k):
        rows = [picked[((h * 2 + u) * 2 + k) * TOK :][:TOK] for h in range(2)]
        value = jnp.concatenate([r[:, :width] for r in rows], 1)
        return value, rows[0][:, width : width + 1] + rows[1][:, width : width + 1]

    def gates(stat):
        affin = [stat[:, 0:1], stat[:, 1:2]]
        total = affin[0] + affin[1]
        return affin, total, [routed_scale * a / total for a in affin]

    _, _, g = gates(x_stat)
    layer_out = x + (g[0] * taken(0, 0)[0] + g[1] * taken(0, 1)[0])
    affin, total, g = gates(s_stat)
    inverse = s_stat[:, 2:3]
    back0, dg0 = taken(1, 0)
    back1, dg1 = taken(1, 1)
    inner = g[0] * dg0 + g[1] * dg1
    grad_normed = g[0] * back0 + g[1] * back1
    grad_logit = [
        routed_scale / total * (dg - inner / routed_scale) * a * (1.0 - a)
        for dg, a in zip((dg0, dg1), affin)
    ]
    for e in range(EXPERTS):
        share = jnp.where(bid[:, 0:1] == e, grad_logit[0], 0.0)
        share = share + jnp.where(bid[:, 1:2] == e, grad_logit[1], 0.0)
        grad_normed = grad_normed + share * router_rows[e : e + 1]
    scaled = grad_normed * gain
    mean = jnp.mean(scaled * s, -1, keepdims=True)
    grad = cot + inverse * scaled - s * inverse * inverse * inverse * mean
    return layer_out.astype(bf16), grad.astype(bf16)


def combine_first_kernel(
    in_ref, x_ref, s_ref, c_ref, stat_ref, fid_ref, bid_ref, gain_ref, router_ref, y_ref, b_ref
):
    y, b = combine(
        in_ref, x_ref[0].astype(f32), s_ref[0, 0].astype(f32), c_ref[0].astype(f32),
        stat_ref[0], stat_ref[1], fid_ref[0, 0], bid_ref[0, 0],
        gain_ref[...].astype(f32), router_ref[...],
    )
    y_ref[...] = y
    b_ref[...] = b


def combine_second_kernel(
    in_ref, x_ref, s_ref, c_ref, stat_ref, x_stat_ref, fid_ref, bid_ref, gain_ref, router_ref,
    y0_ref, b0_ref, y_ref, b_ref,
):
    y, b = combine(
        in_ref, x_ref[...].astype(f32), s_ref[1, 0].astype(f32), c_ref[...].astype(f32),
        x_stat_ref[...], stat_ref[2], fid_ref[1, 0], bid_ref[1, 0],
        gain_ref[...].astype(f32), router_ref[...],
    )
    y_ref[0, 0] = y0_ref[...]
    b_ref[0, 0] = b0_ref[...]
    y_ref[1, 0] = y
    b_ref[1, 0] = b


def call(kernel, outs, *args, smem=0):
    spec = pl.BlockSpec(memory_space=pltpu.VMEM)
    first = pl.BlockSpec(memory_space=pltpu.SMEM)
    outs = [jax.ShapeDtypeStruct(*o) for o in outs]
    return pl.pallas_call(
        kernel,
        out_shape=outs,
        in_specs=[first] * smem + [spec] * (len(args) - smem),
        out_specs=[spec] * len(outs),
        compiler_params=pltpu.CompilerParams(vmem_limit_bytes=48 * 2**20),
    )(*args)


def swapped(block):
    return lax.ppermute(block, "core", [(0, 1), (1, 0)])


def exchanged(block):
    return lax.all_to_all(block, ("x", "y"), split_axis=0, concat_axis=0, tiled=True)


def shifted(block, distance):
    count = lax.axis_size("pipe")
    route_ = [(i - distance, i) for i in range(count) if 0 <= i - distance < count]
    return lax.ppermute(block, "pipe", route_)


def per_device(
    forward_in, forward_new, grad_in, grad_new, saved_inputs, forward_ids, backward_ids,
    norm_gain, router, gate_proj, up_proj, down_proj,
):
    width = forward_in.shape[-1]
    row = (TOK, width)
    stat = (TOK, 128)
    sent, stats = call(
        prepare_kernel,
        [((ROWS, width), bf16), ((3, *stat), f32)],
        forward_in, saved_inputs, grad_in, norm_gain, router, forward_ids, backward_ids,
    )
    gates_, ups, downs = gate_proj[0], up_proj[0], down_proj[0]
    gate_up = jnp.concatenate([gates_, swapped(gates_), ups, swapped(ups)], 1)
    down = jnp.concatenate([downs, swapped(downs)], 0)
    router_rows = router[0].T.astype(f32)
    hidden = gate_up.shape[1]
    packed = (ROWS, width // 2 + PACK)

    came = exchanged(sent)
    sent, keep = call(
        experts_first_kernel, [(packed, bf16), ((ROWS, hidden), f32)], came, gate_up, down
    )
    came = exchanged(sent)
    y0, b0 = call(
        combine_first_kernel, [(row, bf16)] * 2,
        came, forward_in, saved_inputs, grad_in, stats, forward_ids, backward_ids, norm_gain, router_rows,
    )
    section = lax.axis_index("pipe").astype(jnp.int32).reshape(1, 1)
    sent, x1, c1, x1_stat = call(
        functools.partial(again_kernel, last=lax.axis_size("pipe") - 1),
        [((ROWS, width // 2), bf16), (row, bf16), (row, bf16), (stat, f32)],
        section, shifted(y0, 1), forward_new, shifted(b0, -1), grad_new, norm_gain, router,
        forward_ids, backward_ids,
        smem=1,
    )
    came = exchanged(sent)
    (sent,) = call(experts_second_kernel, [(packed, bf16)], came, keep, gate_up, down)
    came = exchanged(sent)
    full = (2, 1, *row)
    return tuple(
        call(
            combine_second_kernel, [(full, bf16)] * 2,
            came, x1, saved_inputs, c1, stats, x1_stat, forward_ids, backward_ids, norm_gain, router_rows,
            y0, b0,
        )
    )


def solution(mesh):
    split = Mesh(np.asarray(mesh.devices).reshape(-1, 4, 4, 2), ("pipe", "x", "y", "core"))
    tokens = ("x", "y", "core")
    in_specs = (
        P("pipe", tokens, None),
        P(None, tokens, None),
        P("pipe", tokens, None),
        P(None, tokens, None),
        P(None, "pipe", tokens, None),
        P(None, "pipe", tokens, None),
        P(None, "pipe", tokens, None),
        P("pipe", None),
        P("pipe", None, None),
        P("pipe", None, tokens),
        P("pipe", None, tokens),
        P("pipe", tokens, None),
    )
    out_specs = (P(None, "pipe", tokens, None), P(None, "pipe", tokens, None))
    return jax.shard_map(
        per_device, mesh=split, in_specs=in_specs, out_specs=out_specs, check_vma=False
    )
```

profile of v0, /device:TPU:224, one launch (start us, length us, event | category | flops | bytes accessed | tf_op | source)
XLA Modules:
  0.0 156.8 jit_solution(10019420386023541631)
XLA Ops:
  0.6 0.8 copy.15.fid_ref
  1.4 0.8 copy.16.bid_ref
  2.2 1.3 copy.14.router_ref
  3.5 0.0 copy-start.2
  3.5 0.9 copy-done.2
  4.4 0.8 copy-done.6
  5.2 0.8 copy-done.8
  6.1 0.7 copy-done.10
  6.8 1.3 shard_map.131
  8.1 0.0 copy-start
  8.1 1.6 %copy-done = bf16[384,3584]{1,0:T(8,128)(2,1)} copy-done((bf16[384,3584]{1,0:T(8,128)(2,1)}, bf16[384,3584]{1,0:T(8,128)(2,1)S(1)}, u32[]{:S(2)}) %copy-start) | copy-done | bytes 2752536
  9.7 7.1 %all-to-all-start = ((bf16[16,24,3584]{2,1,0:T(8,128)(2,1)}), bf16[16,24,3584]{2,1,0:T(8,128)(2,1)}, u32[]{:S(2)}, u32[]{:S(2)}) async-start(bf16[16,24,3584]{2,1,0:T(8,128)(2,1)} %bitcast.20), calls=%async_computation | async-start | bytes 5505024 | tf_op jit(solution)/shard_map/all_to_all | solution.py:274
  16.8 0.0 copy-done.14
  16.8 1.9 %collective-permute-start.2 = (bf16[128,3584]{1,0:T(8,128)(2,1)S(1)}, bf16[128,3584]{1,0:T(8,128)(2,1)S(1)}, u32[]{:S(2)}, u32[]{:S(2)}) collective-permute-start(bf16[128,3584]{1,0:T(8,128)(2,1)S(1)} %bitcast.24), channel_id=1, source_target_pairs={{0,1},{1,0},{2,3},{3,2},{4,5},{5,4},{6,7},{7,6},{8,9},{9,8},{10,11... | collective-permute-start | bytes 2752520 | tf_op jit(solution)/shard_map/ppermute | solution.py:270
  18.7 2.4 %collective-permute-start = (bf16[3584,128]{1,0:T(8,128)(2,1)}, bf16[3584,128]{1,0:T(8,128)(2,1)S(1)}, u32[]{:S(2)}, u32[]{:S(2)}) collective-permute-start(bf16[3584,128]{1,0:T(8,128)(2,1)} %bitcast.3), channel_id=1, source_target_pairs={{0,1},{1,0},{2,3},{3,2},{4,5},{5,4},{6,7},{7,6},{8,9},{9,8},{10,11... | collective-permute-start | bytes 2752520 | tf_op jit(solution)/shard_map/ppermute | solution.py:270
  21.1 1.9 %collective-permute-start.1 = (bf16[3584,128]{1,0:T(8,128)(2,1)}, bf16[3584,128]{1,0:T(8,128)(2,1)S(1)}, u32[]{:S(2)}, u32[]{:S(2)}) collective-permute-start(bf16[3584,128]{1,0:T(8,128)(2,1)} %bitcast.4), channel_id=1, source_target_pairs={{0,1},{1,0},{2,3},{3,2},{4,5},{5,4},{6,7},{7,6},{8,9},{9,8},{10,11... | collective-permute-start | bytes 2752520 | tf_op jit(solution)/shard_map/ppermute | solution.py:270
  23.1 0.0 collective-permute-done.2
  23.1 1.3 pad_maximum_fusion.1.down_ref
  24.4 0.0 collective-permute-done
  24.4 1.3 collective-permute-done.1
  25.7 3.1 %pad_maximum_fusion.gu_ref = bf16[3584,512]{1,0:T(8,128)(2,1)} fusion(bf16[3584,128]{1,0:T(8,128)(2,1)S(1)} %collective-permute-done.1, bf16[3584,128]{1,0:T(8,128)(2,1)} %bitcast.4, bf16[3584,128]{1,0:T(8,128)(2,1)S(1)} %collective-permute-done, bf16[3584,128]{1,0:T(8,128)(2,1)} %bitcast.3), kind=kLoop, calls=%fused_computation | loop fusion | flops 14680064 | bytes 7340032 | tf_op jit(solution)/shard_map/concatenate | solution.py:296
  28.9 26.5 %all-to-all-done = bf16[16,24,3584]{2,1,0:T(8,128)(2,1)} async-done(((bf16[16,24,3584]{2,1,0:T(8,128)(2,1)}), bf16[16,24,3584]{2,1,0:T(8,128)(2,1)}, u32[]{:S(2)}, u32[]{:S(2)}) %all-to-all-start) | async-done | bytes 2752544 | tf_op jit(solution)/shard_map/all_to_all | solution.py:274
  55.4 0.0 copy-start.11
  55.4 8.8 %shard_map.132 = (bf16[384,1920]{1,0:T(8,128)(2,1)S(1)}, f32[384,512]{1,0:T(8,128)S(1)}) custom-call(bf16[384,3584]{1,0:T(8,128)(2,1)} %bitcast.2.in_ref, bf16[3584,512]{1,0:T(8,128)(2,1)} %pad_maximum_fusion.gu_ref, bf16[256,3584]{1,0:T(8,128)(2,1)S(1)} %pad_maximum_fusion.1.down_ref), custom_call_target="tpu_custom_call" | custom-call | tf_op jit(solution)/shard_map/pallas_call | solution.py:260
  64.2 0.0 copy-start.1
  64.2 1.1 copy-done.1
  65.4 0.9 copy-done.4
  66.2 5.2 %all-to-all-start.1 = ((bf16[16,24,1920]{2,1,0:T(8,128)(2,1)}), bf16[16,24,1920]{2,1,0:T(8,128)(2,1)}, u32[]{:S(2)}, u32[]{:S(2)}) async-start(bf16[16,24,1920]{2,1,0:T(8,128)(2,1)} %bitcast.21), calls=%async_computation.1 | async-start | bytes 2949120 | tf_op jit(solution)/shard_map/all_to_all | solution.py:274
  71.4 0.0 copy-done.15
  71.5 20.9 %all-to-all-done.1 = bf16[16,24,1920]{2,1,0:T(8,128)(2,1)} async-done(((bf16[16,24,1920]{2,1,0:T(8,128)(2,1)}), bf16[16,24,1920]{2,1,0:T(8,128)(2,1)}, u32[]{:S(2)}, u32[]{:S(2)}) %all-to-all-start.1) | async-done | bytes 1474592 | tf_op jit(solution)/shard_map/all_to_all | solution.py:274
  92.3 0.0 copy-done.3
  92.3 0.0 copy-done.7
  92.4 0.0 copy-done.9
  92.4 0.0 copy-done.11
  92.4 2.4 %shard_map.133 = (bf16[8,3584]{1,0:T(8,128)(2,1)S(1)}, bf16[8,3584]{1,0:T(8,128)(2,1)S(1)}) custom-call(bf16[384,1920]{1,0:T(8,128)(2,1)} %bitcast.7.in_ref, bf16[1,8,3584]{2,1,0:T(8,128)(2,1)S(1)} %copy-done.7, bf16[2,1,8,3584]{3,2,1,0:T(8,128)(2,1)S(1)} %copy-done.3, bf16[1,8,3584]{2,1,0:T(8,128)(2,1)S(1)} %copy-done.9, ...), custom_call_target="tpu_custom_call" | custom-call | tf_op jit(solution)/shard_map/pallas_call | solution.py:260
  94.8 5.1 %collective-permute-start.3 = (bf16[8,3584]{1,0:T(8,128)(2,1)S(1)}, bf16[8,3584]{1,0:T(8,128)(2,1)S(1)}, u32[]{:S(2)}, u32[]{:S(2)}) collective-permute-start(bf16[8,3584]{1,0:T(8,128)(2,1)S(1)} %get-tuple-element.15.y0_ref), channel_id=1, source_target_pairs={{0,32},{32,64},{64,96},{96,128},{128,160},{160,192},{192,224},{224... | collective-permute-start | bytes 172040 | tf_op jit(solution)/shard_map/ppermute | solution.py:280
  99.9 1.9 %collective-permute-start.4 = (bf16[8,3584]{1,0:T(8,128)(2,1)S(1)}, bf16[8,3584]{1,0:T(8,128)(2,1)S(1)}, u32[]{:S(2)}, u32[]{:S(2)}) collective-permute-start(bf16[8,3584]{1,0:T(8,128)(2,1)S(1)} %get-tuple-element.16.b0_ref), channel_id=1, source_target_pairs={{32,0},{64,32},{96,64},{128,96},{160,128},{192,160},{224,192},{256... | collective-permute-start | bytes 172040 | tf_op jit(solution)/shard_map/ppermute | solution.py:280
  101.8 0.0 copy-start.5
  101.8 0.0 collective-permute-done.3.y_ref
  101.8 5.3 %collective-permute-done.4.b_ref = bf16[8,3584]{1,0:T(8,128)(2,1)S(1)} collective-permute-done((bf16[8,3584]{1,0:T(8,128)(2,1)S(1)}, bf16[8,3584]{1,0:T(8,128)(2,1)S(1)}, u32[]{:S(2)}, u32[]{:S(2)}) %collective-permute-start.4) | collective-permute-done | bytes 57376 | tf_op jit(solution)/shard_map/ppermute | solution.py:280
  107.1 0.0 copy-done.12
  107.1 0.0 copy-done.13
  107.1 0.7 shard_map.134
  107.9 20.2 %all_to_all.44 = bf16[16,24,1792]{2,1,0:T(8,128)(2,1)S(1)} all-to-all(bf16[16,24,1792]{2,1,0:T(8,128)(2,1)S(1)} %bitcast.22), channel_id=1, replica_groups=mesh['pipe'=16,'x'=4,'y'=4,'core'=2] {'x','y'}, dimensions={0} | all-to-all | bytes 2752512 | tf_op jit(solution)/shard_map/all_to_all | solution.py:274
  128.1 0.0 copy-done.5
  128.1 6.8 %shard_map.135 = bf16[384,1920]{1,0:T(8,128)(2,1)S(1)} custom-call(bf16[384,1792]{1,0:T(8,128)(2,1)S(1)} %bitcast.19, f32[384,512]{1,0:T(8,128)S(1)} %copy-done.5, bf16[3584,512]{1,0:T(8,128)(2,1)} %pad_maximum_fusion.gu_ref, bf16[256,3584]{1,0:T(8,128)(2,1)S(1)} %pad_maximum_fusion.1.down_ref), custom_call_target="tpu_custom_call" | custom-call | tf_op jit(solution)/shard_map/pallas_call | solution.py:260
  134.9 20.2 %all_to_all.45 = bf16[16,24,1920]{2,1,0:T(8,128)(2,1)S(1)} all-to-all(bf16[16,24,1920]{2,1,0:T(8,128)(2,1)S(1)} %bitcast.17), channel_id=1, replica_groups=mesh['pipe'=16,'x'=4,'y'=4,'core'=2] {'x','y'}, dimensions={0} | all-to-all | bytes 2949120 | tf_op jit(solution)/shard_map/all_to_all | solution.py:274
  155.1 1.7 %shard_map.136 = (bf16[2,1,8,3584]{3,2,1,0:T(8,128)(2,1)}, bf16[2,1,8,3584]{3,2,1,0:T(8,128)(2,1)}) custom-call(bf16[384,1920]{1,0:T(8,128)(2,1)S(1)} %bitcast.18, bf16[8,3584]{1,0:T(8,128)(2,1)S(1)} %get-tuple-element.19.x_ref, bf16[2,1,8,3584]{3,2,1,0:T(8,128)(2,1)S(1)} %copy-done.3, bf16[8,3584]{1,0:T(8,128)(2,1)S(1)} %get-tuple-element.20.c_ref, ...), custom_call_target="tpu_custom_call" | custom-call | tf_op jit(solution)/shard_map/pallas_call | solution.py:260
  (12 shorter events, 0.0 us)
Async XLA Ops:
  2.2 14.6 %copy-start.14 = (bf16[1,128,3584]{2,1,0:T(8,128)(2,1)S(1)}, bf16[1,128,3584]{2,1,0:T(8,128)(2,1)}, u32[]{:S(2)}) copy-start(bf16[1,128,3584]{2,1,0:T(8,128)(2,1)} %param.23) | copy-start | bytes 2752516
  3.5 0.9 copy-start.2
  4.4 0.8 copy-start.6
  5.2 0.8 copy-start.8
  6.1 0.7 copy-start.10
  8.1 1.6 %copy-start = (bf16[384,3584]{1,0:T(8,128)(2,1)}, bf16[384,3584]{1,0:T(8,128)(2,1)S(1)}, u32[]{:S(2)}) copy-start(bf16[384,3584]{1,0:T(8,128)(2,1)S(1)} %get-tuple-element.12) | copy-start | bytes 8257540
  9.7 45.7 %all-to-all-start = ((bf16[16,24,3584]{2,1,0:T(8,128)(2,1)}), bf16[16,24,3584]{2,1,0:T(8,128)(2,1)}, u32[]{:S(2)}, u32[]{:S(2)}) async-start(bf16[16,24,3584]{2,1,0:T(8,128)(2,1)} %bitcast.20), calls=%async_computation | async-start | bytes 5505024 | tf_op jit(solution)/shard_map/all_to_all | solution.py:274
  16.8 6.3 %collective-permute-start.2 = (bf16[128,3584]{1,0:T(8,128)(2,1)S(1)}, bf16[128,3584]{1,0:T(8,128)(2,1)S(1)}, u32[]{:S(2)}, u32[]{:S(2)}) collective-permute-start(bf16[128,3584]{1,0:T(8,128)(2,1)S(1)} %bitcast.24), channel_id=1, source_target_pairs={{0,1},{1,0},{2,3},{3,2},{4,5},{5,4},{6,7},{7,6},{8,9},{9,8},{10,11... | collective-permute-start | bytes 2752520 | tf_op jit(solution)/shard_map/ppermute | solution.py:270
  18.7 5.7 %collective-permute-start = (bf16[3584,128]{1,0:T(8,128)(2,1)}, bf16[3584,128]{1,0:T(8,128)(2,1)S(1)}, u32[]{:S(2)}, u32[]{:S(2)}) collective-permute-start(bf16[3584,128]{1,0:T(8,128)(2,1)} %bitcast.3), channel_id=1, source_target_pairs={{0,1},{1,0},{2,3},{3,2},{4,5},{5,4},{6,7},{7,6},{8,9},{9,8},{10,11... | collective-permute-start | bytes 2752520 | tf_op jit(solution)/shard_map/ppermute | solution.py:270
  21.1 4.6 %collective-permute-start.1 = (bf16[3584,128]{1,0:T(8,128)(2,1)}, bf16[3584,128]{1,0:T(8,128)(2,1)S(1)}, u32[]{:S(2)}, u32[]{:S(2)}) collective-permute-start(bf16[3584,128]{1,0:T(8,128)(2,1)} %bitcast.4), channel_id=1, source_target_pairs={{0,1},{1,0},{2,3},{3,2},{4,5},{5,4},{6,7},{7,6},{8,9},{9,8},{10,11... | collective-permute-start | bytes 2752520 | tf_op jit(solution)/shard_map/ppermute | solution.py:270
  55.4 16.1 %copy-start.15 = (bf16[1,3584,4]{1,2,0:T(4,128)(2,1)S(1)}, bf16[1,3584,4]{1,2,0:T(4,128)(2,1)}, u32[]{:S(2)}) copy-start(bf16[1,3584,4]{1,2,0:T(4,128)(2,1)} %param.20) | copy-start | bytes 86020
  55.4 37.0 %copy-start.3 = (bf16[2,1,8,3584]{3,2,1,0:T(8,128)(2,1)S(1)}, bf16[2,1,8,3584]{3,2,1,0:T(8,128)(2,1)}, u32[]{:S(2)}) copy-start(bf16[2,1,8,3584]{3,2,1,0:T(8,128)(2,1)} %s_ref.5) | copy-start | bytes 344068
  55.4 37.0 %copy-start.7 = (bf16[1,8,3584]{2,1,0:T(8,128)(2,1)S(1)}, bf16[1,8,3584]{2,1,0:T(8,128)(2,1)}, u32[]{:S(2)}) copy-start(bf16[1,8,3584]{2,1,0:T(8,128)(2,1)} %x_ref.3) | copy-start | bytes 172036
  55.4 37.0 %copy-start.9 = (bf16[1,8,3584]{2,1,0:T(8,128)(2,1)S(1)}, bf16[1,8,3584]{2,1,0:T(8,128)(2,1)}, u32[]{:S(2)}) copy-start(bf16[1,8,3584]{2,1,0:T(8,128)(2,1)} %c_ref.3) | copy-start | bytes 172036
  55.4 37.0 %copy-start.11 = (bf16[1,3584]{1,0:T(2,128)(2,1)S(1)}, bf16[1,3584]{1,0:T(2,128)(2,1)}, u32[]{:S(2)}) copy-start(bf16[1,3584]{1,0:T(2,128)(2,1)} %gain_ref.7) | copy-start | bytes 21508
  64.2 1.1 copy-start.1
  65.4 0.9 copy-start.4
  66.2 40.9 %copy-start.12 = (bf16[1,8,3584]{2,1,0:T(8,128)(2,1)S(1)}, bf16[1,8,3584]{2,1,0:T(8,128)(2,1)}, u32[]{:S(2)}) copy-start(bf16[1,8,3584]{2,1,0:T(8,128)(2,1)} %fnew_ref.1) | copy-start | bytes 172036
  66.2 40.9 %copy-start.13 = (bf16[1,8,3584]{2,1,0:T(8,128)(2,1)S(1)}, bf16[1,8,3584]{2,1,0:T(8,128)(2,1)}, u32[]{:S(2)}) copy-start(bf16[1,8,3584]{2,1,0:T(8,128)(2,1)} %gnew_ref.1) | copy-start | bytes 172036
  66.2 26.1 %all-to-all-start.1 = ((bf16[16,24,1920]{2,1,0:T(8,128)(2,1)}), bf16[16,24,1920]{2,1,0:T(8,128)(2,1)}, u32[]{:S(2)}, u32[]{:S(2)}) async-start(bf16[16,24,1920]{2,1,0:T(8,128)(2,1)} %bitcast.21), calls=%async_computation.1 | async-start | bytes 2949120 | tf_op jit(solution)/shard_map/all_to_all | solution.py:274
  94.8 7.0 %collective-permute-start.3 = (bf16[8,3584]{1,0:T(8,128)(2,1)S(1)}, bf16[8,3584]{1,0:T(8,128)(2,1)S(1)}, u32[]{:S(2)}, u32[]{:S(2)}) collective-permute-start(bf16[8,3584]{1,0:T(8,128)(2,1)S(1)} %get-tuple-element.15.y0_ref), channel_id=1, source_target_pairs={{0,32},{32,64},{64,96},{96,128},{128,160},{160,192},{192,224},{224... | collective-permute-start | bytes 172040 | tf_op jit(solution)/shard_map/ppermute | solution.py:280
  99.9 7.3 %collective-permute-start.4 = (bf16[8,3584]{1,0:T(8,128)(2,1)S(1)}, bf16[8,3584]{1,0:T(8,128)(2,1)S(1)}, u32[]{:S(2)}, u32[]{:S(2)}) collective-permute-start(bf16[8,3584]{1,0:T(8,128)(2,1)S(1)} %get-tuple-element.16.b0_ref), channel_id=1, source_target_pairs={{32,0},{64,32},{96,64},{128,96},{160,128},{192,160},{224,192},{256... | collective-permute-start | bytes 172040 | tf_op jit(solution)/shard_map/ppermute | solution.py:280
  101.8 26.3 %copy-start.5 = (f32[384,512]{1,0:T(8,128)S(1)}, f32[384,512]{1,0:T(8,128)}, u32[]{:S(2)}) copy-start(f32[384,512]{1,0:T(8,128)} %copy-done.4) | copy-start | bytes 2359300
where the time goes:
time: 158 us; the launch traced here: 157 us
  waiting for transfers between devices  54.1 us (34%)
  blocking collectives  40.4 us (26%)
  starting transfers between devices  25.5 us (16%)
  Pallas kernels  21.8 us (14%)
  local copies, waits for them, and re-layouts  9.73 us (6%)
  other arithmetic  4.45 us (3%)
    all_to_all x2, waiting for transfers between devices, exchanged(): lax.all_to_all(block, ('x', 'y'), split_axis=0, concat_axis=0, tiled=True)  47.4 us
    all_to_all x2, blocking collectives, exchanged(): lax.all_to_all(block, ('x', 'y'), split_axis=0, concat_axis=0, tiled=True)  40.4 us
    pallas_call x6, Pallas kernels, call(): pl.pallas_call(kernel, out_shape=outs, in_specs=[first] * smem + [spec] *...  21.8 us
    all_to_all x2, starting transfers between devices, exchanged(): lax.all_to_all(block, ('x', 'y'), split_axis=0, concat_axis=0, tiled=True)  12.3 us
    unnamed x35, local copies, waits for them, and re-layouts  9.73 us
    ppermute x2, starting transfers between devices, shifted(): return lax.ppermute(block, 'pipe', route_)  6.99 us
    ppermute x3, starting transfers between devices, swapped(): return lax.ppermute(block, 'core', [(0, 1), (1, 0)])  6.25 us
    ppermute x2, waiting for transfers between devices, shifted(): return lax.ppermute(block, 'pipe', route_)  5.33 us
  transfers between devices with their start and end apart: 7, of which 4 were waited for; matrix products, arithmetic and copies ran while one was open for 3% of the time, Pallas kernels for 0%

commit v1 on v0

--- a/solution.py
+++ b/solution.py
@@ -50,12 +50,17 @@
     return expert, unit, offset - CAP * unit
 
 
-def tables(ids):
-    cols = jnp.concatenate([u.astype(f32) for u in ids], 0)
-    n = cols.shape[0]
+def columns(ids):
+    wide = ids.astype(f32)
+    here = iota((TOK, TOK), 0) == iota((TOK, TOK), 1)
+    return [jnp.sum(jnp.where(here, wide[k : k + 1], 0.0), 1, keepdims=True) for k in range(2)]
+
+
+def tables(choices):
+    col = [jnp.concatenate([c[k] for c in choices], 0) for k in range(2)]
+    n = col[0].shape[0]
     i, j = iota((n, n), 0), iota((n, n), 1)
     same = whole(i, TOK) == whole(j, TOK)
-    col = [cols[:, k : k + 1] for k in range(2)]
     lane = [jnp.sum(jnp.where(i == j, c, 0.0), 0, keepdims=True) for c in col]
     col_pos, lane_pos = [], []
     for k in range(2):
@@ -66,15 +71,13 @@
     return col, col_pos, lane, lane_pos
 
 
-def dispatch(rows, ids):
-    _, _, lane, lane_pos = tables(ids)
+def dispatch_table(choices):
+    _, _, lane, lane_pos = tables(choices)
     shape = (ROWS, UNITS * TOK)
     expert, unit, slot = row_codes(shape, 0)
     hit = (expert == lane[0]) & (slot == lane_pos[0]) | (expert == lane[1]) & (slot == lane_pos[1])
     hit = hit & (unit == whole(iota(shape, 1), TOK))
-    table = jnp.where(hit, 1.0, 0.0).astype(bf16)
-    stacked = jnp.concatenate(rows, 0).astype(bf16)
-    return dot(table, stacked).astype(bf16)
+    return jnp.where(hit, 1.0, 0.0)
 
 
 def norm_rows(wide, gain):
@@ -82,28 +85,48 @@
     return inverse, (wide * inverse * gain).astype(bf16).astype(f32)
 
 
-def route(normed, inverse, ids, router):
-    logits = dot(normed.astype(bf16), router)
-    lanes = iota(logits.shape, 1)
+def route(normed, inverse, choice, router):
+    logits = dot_nt(normed.astype(bf16), router)
+    lanes = iota(logits.shape, 1).astype(f32)
     affin = [
-        jax.nn.sigmoid(jnp.sum(jnp.where(lanes == ids[:, k : k + 1], logits, 0.0), -1, keepdims=True))
+        jax.nn.sigmoid(jnp.sum(jnp.where(lanes == choice[k], logits, 0.0), -1, keepdims=True))
         for k in range(2)
     ]
     at = iota((TOK, 128), 1)
     return jnp.where(at == 0, affin[0], jnp.where(at == 1, affin[1], inverse))
 
 
-def prepare_kernel(x_ref, s_ref, c_ref, gain_ref, router_ref, fid_ref, bid_ref, out_ref, stat_ref):
+def prepare_kernel(
+    x_hbm, s_hbm, c_hbm, gain_hbm, router_hbm, fid_hbm, bid_hbm, out_hbm, stat_ref,
+    x_ref, s_ref, c_ref, gain_ref, router_ref, fid_ref, bid_ref, out_ref, in_sem, out_sem,
+):
+    sources = (fid_hbm, bid_hbm, x_hbm, s_hbm, gain_hbm, router_hbm, c_hbm)
+    places = (fid_ref, bid_ref, x_ref, s_ref, gain_ref, router_ref, c_ref)
+    fetches = [pltpu.make_async_copy(a, b, in_sem.at[n]) for n, (a, b) in enumerate(zip(sources, places))]
+    for fetch in fetches:
+        fetch.start()
+    fetches[0].wait()
+    fetches[1].wait()
+    choices = [columns(ids) for ids in (fid_ref[0, 0], bid_ref[0, 0], bid_ref[1, 0])]
+    table = dispatch_table([choices[0], choices[1], choices[1], choices[2]])
+    for fetch in fetches[2:]:
+        fetch.wait()
     gain = gain_ref[...].astype(f32)
-    router = router_ref[0]
-    ids = [fid_ref[0, 0], bid_ref[0, 0], bid_ref[1, 0]]
     rows = []
     for n, wide in enumerate((x_ref[0], s_ref[0, 0], s_ref[1, 0])):
         inverse, normed = norm_rows(wide.astype(f32), gain)
-        stat_ref[n] = route(normed, inverse, ids[n], router)
+        stat_ref[n] = route(normed, inverse, choices[n], router_ref[...])
         rows.append(normed)
-    units = [rows[0], rows[1], c_ref[0].astype(f32), rows[2]]
-    out_ref[...] = dispatch(units, [ids[0], ids[1], ids[1], ids[2]])
+    stacked = jnp.concatenate([rows[0], rows[1], c_ref[0].astype(f32), rows[2]], 0).astype(bf16)
+    step = ROWS // EXPERTS
+    sends = []
+    for e in range(EXPERTS):
+        at = pl.ds(e * step, step)
+        out_ref[at] = dot(table[e * step : (e + 1) * step].astype(bf16), stacked).astype(bf16)
+        sends.append(pltpu.make_async_copy(out_ref.at[at], out_hbm.at[at], out_sem.at[e]))
+        sends[-1].start()
+    for send in sends:
+        send.wait()
 
 
 def again_kernel(
@@ -116,12 +139,13 @@
     c = jnp.where(final, gnew_ref[0].astype(f32), b_ref[...].astype(f32))
     x_ref[...] = x.astype(bf16)
     c_ref[...] = c.astype(bf16)
-    ids = [fid_ref[1, 0], bid_ref[1, 0]]
+    choices = [columns(fid_ref[1, 0]), columns(bid_ref[1, 0])]
     inverse, normed = norm_rows(x, gain_ref[...].astype(f32))
-    stat_ref[...] = route(normed, inverse, ids[0], router_ref[0])
+    stat_ref[...] = route(normed, inverse, choices[0], router_ref[...])
     half = x.shape[1] // 2
     units = [normed[:, :half], c[:, :half], normed[:, half:], c[:, half:]]
-    out_ref[...] = dispatch(units, ids + ids)
+    table = dispatch_table(choices + choices).astype(bf16)
+    out_ref[...] = dot(table, jnp.concatenate(units, 0).astype(bf16)).astype(bf16)
 
 
 def roll_up(value, count):
@@ -162,17 +186,73 @@
     out_ref[:, width : width + PACK] = jnp.where(left[:, :PACK], high, low).astype(bf16)
 
 
-def experts_first_kernel(in_ref, gu_ref, down_ref, out_ref, keep_ref):
-    pre = dot(in_ref[...], gu_ref[...])
+CHUNKS = 4
+
+
+class Weights:
+    def __init__(self, w_hbm, gu_ref, down_ref, sems):
+        depth, width = w_hbm[0].shape[1:]
+        self.chunk = depth // CHUNKS
+        self.groups = []
+        for n in range(CHUNKS):
+            at = pl.ds(n * self.chunk, self.chunk)
+            self.groups.append(
+                [
+                    pltpu.make_async_copy(
+                        w_hbm[i].at[0, at, :], gu_ref.at[at, i * width : (i + 1) * width], sems.at[n * 4 + i]
+                    )
+                    for i in range(4)
+                ]
+            )
+        self.groups.append(
+            [
+                pltpu.make_async_copy(
+                    w_hbm[4 + i].at[0], down_ref.at[i * width : (i + 1) * width, :], sems.at[CHUNKS * 4 + i]
+                )
+                for i in range(2)
+            ]
+        )
+        self.start(0)
+        self.start(1)
+
+    def start(self, n):
+        if n < len(self.groups):
+            for copy in self.groups[n]:
+                copy.start()
+
+    def wait(self, n):
+        for copy in self.groups[n]:
+            copy.wait()
+        self.start(n + 2)
+
+
+def experts_first_kernel(in_ref, *refs):
+    w_hbm, (out_ref, keep_ref, gu_ref, down_ref, sems) = refs[:6], refs[6:]
+    weights = Weights(w_hbm, gu_ref, down_ref, sems)
+    pre = 0.0
+    for n in range(CHUNKS):
+        weights.wait(n)
+        at = slice(n * weights.chunk, (n + 1) * weights.chunk)
+        pre = pre + dot(in_ref[:, at], gu_ref[at, :])
+    keep_ref[...] = roll_up(pre, 2 * CAP)
+    weights.wait(CHUNKS)
     grad_act = roll_up(dot_nt(in_ref[...], down_ref[...]), CAP)
-    keep_ref[...] = roll_up(pre, 2 * CAP)
     experts(pre, grad_act, gu_ref, down_ref, out_ref)
 
 
-def experts_second_kernel(in_ref, keep_ref, gu_ref, down_ref, out_ref):
+def experts_second_kernel(in_ref, keep_ref, *refs):
+    w_hbm, (out_ref, gu_ref, down_ref, sems) = refs[:6], refs[6:]
+    weights = Weights(w_hbm, gu_ref, down_ref, sems)
     width = in_ref.shape[1]
+    sides = [0.0, 0.0]
+    for n in range(CHUNKS):
+        weights.wait(n)
+        h, at = divmod(n * weights.chunk, width)
+        part = dot(in_ref[:, at : at + weights.chunk], gu_ref[n * weights.chunk : (n + 1) * weights.chunk, :])
+        sides[h] = sides[h] + part
+    pre = sides[0] + roll_up(sides[1], 2 * CAP)
+    weights.wait(CHUNKS)
     rows = in_ref[...]
-    pre = dot(rows, gu_ref[:width, :]) + roll_up(dot(rows, gu_ref[width:, :]), 2 * CAP)
     grad_act = dot_nt(rows, down_ref[:, :width]) + roll_up(dot_nt(rows, down_ref[:, width:]), 2 * CAP)
     offset = iota((CHIPS, BLOCK, pre.shape[1]), 1).reshape(pre.shape)
     pre = jnp.where(offset < CAP, pre, keep_ref[...])
@@ -180,7 +260,8 @@
 
 
 def combine(in_ref, x, s, cot, x_stat, s_stat, fid, bid, gain, router_rows):
-    col, col_pos, _, _ = tables([fid, bid])
+    choices = [columns(fid), columns(bid)]
+    col, col_pos, _, _ = tables(choices)
     shape = (TOK, ROWS)
     expert, unit, slot = row_codes(shape, 1)
     blocks = []
@@ -217,9 +298,9 @@
         for dg, a in zip((dg0, dg1), affin)
     ]
     for e in range(EXPERTS):
-        share = jnp.where(bid[:, 0:1] == e, grad_logit[0], 0.0)
-        share = share + jnp.where(bid[:, 1:2] == e, grad_logit[1], 0.0)
-        grad_normed = grad_normed + share * router_rows[e : e + 1]
+        share = jnp.where(choices[1][0] == e, grad_logit[0], 0.0)
+        share = share + jnp.where(choices[1][1] == e, grad_logit[1], 0.0)
+        grad_normed = grad_normed + share * router_rows[e : e + 1].astype(f32)
     scaled = grad_normed * gain
     mean = jnp.mean(scaled * s, -1, keepdims=True)
     grad = cot + inverse * scaled - s * inverse * inverse * inverse * mean
@@ -253,17 +334,35 @@
     b_ref[1, 0] = b
 
 
-def call(kernel, outs, *args, smem=0):
+VMEM_BYTES = 28 * 2**20
+PREPARE_BYTES = 62 * 2**20
+
+
+def in_hbm(args):
+    return [pltpu.with_memory_space_constraint(a, pltpu.HBM) for a in args]
+
+
+def call(kernel, outs, *args, smem=0, weights=()):
     spec = pl.BlockSpec(memory_space=pltpu.VMEM)
     first = pl.BlockSpec(memory_space=pltpu.SMEM)
+    far = pl.BlockSpec(memory_space=pltpu.HBM)
     outs = [jax.ShapeDtypeStruct(*o) for o in outs]
+    scratch = []
+    if weights:
+        depth, width = weights[0].shape[1:]
+        scratch = [
+            pltpu.VMEM((depth, 4 * width), bf16),
+            pltpu.VMEM((2 * width, depth), bf16),
+            pltpu.SemaphoreType.DMA((CHUNKS * 4 + 2,)),
+        ]
     return pl.pallas_call(
         kernel,
         out_shape=outs,
-        in_specs=[first] * smem + [spec] * (len(args) - smem),
+        in_specs=[first] * smem + [spec] * (len(args) - smem) + [far] * len(weights),
         out_specs=[spec] * len(outs),
-        compiler_params=pltpu.CompilerParams(vmem_limit_bytes=48 * 2**20),
-    )(*args)
+        scratch_shapes=scratch,
+        compiler_params=pltpu.CompilerParams(vmem_limit_bytes=VMEM_BYTES),
+    )(*args, *in_hbm(weights))
 
 
 def swapped(block):
@@ -287,26 +386,37 @@
     width = forward_in.shape[-1]
     row = (TOK, width)
     stat = (TOK, 128)
-    sent, stats = call(
+    forward_ids = forward_ids.transpose(0, 1, 3, 2)
+    backward_ids = backward_ids.transpose(0, 1, 3, 2)
+    router = router[0].T
+    args = (forward_in, saved_inputs, grad_in, norm_gain, router, forward_ids, backward_ids)
+    sent, stats = pl.pallas_call(
         prepare_kernel,
-        [((ROWS, width), bf16), ((3, *stat), f32)],
-        forward_in, saved_inputs, grad_in, norm_gain, router, forward_ids, backward_ids,
-    )
-    gates_, ups, downs = gate_proj[0], up_proj[0], down_proj[0]
-    gate_up = jnp.concatenate([gates_, swapped(gates_), ups, swapped(ups)], 1)
-    down = jnp.concatenate([downs, swapped(downs)], 0)
-    router_rows = router[0].T.astype(f32)
-    hidden = gate_up.shape[1]
+        out_shape=[jax.ShapeDtypeStruct((ROWS, width), bf16), jax.ShapeDtypeStruct((3, *stat), f32)],
+        in_specs=[pl.BlockSpec(memory_space=pltpu.HBM)] * len(args),
+        out_specs=[pl.BlockSpec(memory_space=pltpu.HBM), pl.BlockSpec(memory_space=pltpu.VMEM)],
+        scratch_shapes=[pltpu.VMEM(a.shape, a.dtype) for a in args]
+        + [
+            pltpu.VMEM((ROWS, width), bf16),
+            pltpu.SemaphoreType.DMA((len(args),)),
+            pltpu.SemaphoreType.DMA((EXPERTS,)),
+        ],
+        compiler_params=pltpu.CompilerParams(vmem_limit_bytes=PREPARE_BYTES),
+    )(*in_hbm(args))
+    weights = []
+    for own in (gate_proj, up_proj, down_proj):
+        weights += [own, swapped(own)]
+    hidden = 4 * gate_proj.shape[-1]
     packed = (ROWS, width // 2 + PACK)
 
     came = exchanged(sent)
     sent, keep = call(
-        experts_first_kernel, [(packed, bf16), ((ROWS, hidden), f32)], came, gate_up, down
+        experts_first_kernel, [(packed, bf16), ((ROWS, hidden), f32)], came, weights=weights
     )
     came = exchanged(sent)
     y0, b0 = call(
         combine_first_kernel, [(row, bf16)] * 2,
-        came, forward_in, saved_inputs, grad_in, stats, forward_ids, backward_ids, norm_gain, router_rows,
+        came, forward_in, saved_inputs, grad_in, stats, forward_ids, backward_ids, norm_gain, router,
     )
     section = lax.axis_index("pipe").astype(jnp.int32).reshape(1, 1)
     sent, x1, c1, x1_stat = call(
@@ -317,13 +427,13 @@
         smem=1,
     )
     came = exchanged(sent)
-    (sent,) = call(experts_second_kernel, [(packed, bf16)], came, keep, gate_up, down)
+    (sent,) = call(experts_second_kernel, [(packed, bf16)], came, keep, weights=weights)
     came = exchanged(sent)
     full = (2, 1, *row)
     return tuple(
         call(
             combine_second_kernel, [(full, bf16)] * 2,
-            came, x1, saved_inputs, c1, stats, x1_stat, forward_ids, backward_ids, norm_gain, router_rows,
+            came, x1, saved_inputs, c1, stats, x1_stat, forward_ids, backward_ids, norm_gain, router,
             y0, b0,
         )
     )

time: 158 us -> 147 us (0.930)
  blocking collectives: 40.4 us -> 64.5 us
  waiting for transfers between devices: 54.1 us -> 36 us
  local copies, waits for them, and re-layouts: 9.73 us -> 1.57 us
  starting transfers between devices: 25.5 us -> 20.3 us
  other arithmetic: 4.45 us -> 0 us
  Pallas kernels: 21.8 us -> 23.6 us
    all_to_all x2 -> x3, blocking collectives: 40.4 us -> 64.5 us  [exchanged(): lax.all_to_all(block, ('x', 'y'), split_axis=0, concat_axis=0, tiled=True)]
    all_to_all x2 -> x1, waiting for transfers between devices: 47.4 us -> 29.4 us  [exchanged(): lax.all_to_all(block, ('x', 'y'), split_axis=0, concat_axis=0, tiled=True)]
    unnamed x35 -> x24, local copies, waits for them, and re-layouts: 9.73 us -> 1.57 us
    all_to_all x2 -> x1, starting transfers between devices: 12.3 us -> 7.05 us  [exchanged(): lax.all_to_all(block, ('x', 'y'), split_axis=0, concat_axis=0, tiled=True)]
    concatenate x2 -> x0, other arithmetic: 4.44 us -> none  [the longest x1 3.14 us: per_device(): gate_up = jnp.concatenate([gates_, swapped(gates_), ups, swapped(ups)], 1)]
    pallas_call x0 -> x1, Pallas kernels: none -> 3.86 us  [per_device(): pl.pallas_call(prepare_kernel, out_shape=[jax.ShapeDtypeStruct((ROWS, wid...]
    pallas_call x6 -> x5, Pallas kernels: 21.8 us -> 19.8 us  [call(): pl.pallas_call(kernel, out_shape=outs, in_specs=[first] * smem + [spec] *...]
  transfers between devices with their start and end apart: 7 -> 6, of which waited for: 4 -> 4; matrix products, arithmetic and copies ran while one was open for 3% -> 0% of each run, Pallas kernels for 0% -> 0%
where the time goes in v1:
time: 147 us
  blocking collectives  64.5 us (44%)
  waiting for transfers between devices  36 us (24%)
  Pallas kernels  23.6 us (16%)
  starting transfers between devices  20.3 us (14%)
  local copies, waits for them, and re-layouts  1.57 us (1%)
    all_to_all x3, blocking collectives, exchanged(): lax.all_to_all(block, ('x', 'y'), split_axis=0, concat_axis=0, tiled=True)  64.5 us
    all_to_all x1, waiting for transfers between devices, exchanged(): lax.all_to_all(block, ('x', 'y'), split_axis=0, concat_axis=0, tiled=True)  29.4 us
    pallas_call x5, Pallas kernels, call(): pl.pallas_call(kernel, out_shape=outs, in_specs=[first] * smem + [spec] *...  19.8 us
    all_to_all x1, starting transfers between devices, exchanged(): lax.all_to_all(block, ('x', 'y'), split_axis=0, concat_axis=0, tiled=True)  7.05 us
    ppermute x2, starting transfers between devices, shifted(): return lax.ppermute(block, 'pipe', route_)  6.96 us
    ppermute x3, starting transfers between devices, swapped(): return lax.ppermute(block, 'core', [(0, 1), (1, 0)])  6.25 us
    ppermute x2, waiting for transfers between devices, shifted(): return lax.ppermute(block, 'pipe', route_)  5.34 us
    pallas_call x1, Pallas kernels, per_device(): pl.pallas_call(prepare_kernel, out_shape=[jax.ShapeDtypeStruct((ROWS, wid...  3.86 us
  transfers between devices with their start and end apart: 6, of which 4 were waited for; matrix products, arithmetic and copies ran while one was open for 0% of the time, Pallas kernels for 0%

profile of v1, /device:TPU:224, one launch (start us, length us, event | category | flops | bytes accessed | tf_op | source)
XLA Modules:
  0.0 146.9 jit_solution(936081709464029001)
XLA Ops:
  0.6 3.9 %shard_map.131 = (bf16[384,3584]{1,0:T(8,128)(2,1)}, f32[3,8,128]{2,1,0:T(8,128)}) custom-call(bf16[1,8,3584]{2,1,0:T(8,128)(2,1)} %x_ref.1, bf16[2,1,8,3584]{3,2,1,0:T(8,128)(2,1)} %s_ref.3, bf16[1,8,3584]{2,1,0:T(8,128)(2,1)} %c_ref.1, bf16[1,3584]{1,0:T(2,128)(2,1)} %gain_ref.5, bf16[4,3584]{1,0:T(4,128)(2,1)} %bitcast.21, s32[2,1,2,8]{3,2,1,0:T(2,128)} %bitcast.25, ...), custom_call_target="tpu_custom_call" | custom-call | tf_op jit(solution)/shard_map/pallas_call | solution.py:393
  4.5 7.0 %all-to-all-start = ((bf16[16,24,3584]{2,1,0:T(8,128)(2,1)}), bf16[16,24,3584]{2,1,0:T(8,128)(2,1)S(1)}, u32[]{:S(2)}, u32[]{:S(2)}) async-start(bf16[16,24,3584]{2,1,0:T(8,128)(2,1)} %bitcast.33), calls=%async_computation | async-start | bytes 5505024 | tf_op jit(solution)/shard_map/all_to_all | solution.py:373
  11.6 1.9 %collective-permute-start = (bf16[1,3584,128]{2,1,0:T(8,128)(2,1)}, bf16[1,3584,128]{2,1,0:T(8,128)(2,1)S(1)}, u32[]{:S(2)}, u32[]{:S(2)}) collective-permute-start(bf16[1,3584,128]{2,1,0:T(8,128)(2,1)} %refs_0_.3), channel_id=1, source_target_pairs={{0,1},{1,0},{2,3},{3,2},{4,5},{5,4},{6,7},{7,6},{8,9},{9,8},{10,11... | collective-permute-start | bytes 2752520 | tf_op jit(solution)/shard_map/ppermute | solution.py:369
  13.5 2.4 %collective-permute-start.1 = (bf16[1,3584,128]{2,1,0:T(8,128)(2,1)}, bf16[1,3584,128]{2,1,0:T(8,128)(2,1)S(1)}, u32[]{:S(2)}, u32[]{:S(2)}) collective-permute-start(bf16[1,3584,128]{2,1,0:T(8,128)(2,1)} %refs_2_.3), channel_id=1, source_target_pairs={{0,1},{1,0},{2,3},{3,2},{4,5},{5,4},{6,7},{7,6},{8,9},{9,8},{10,11... | collective-permute-start | bytes 2752520 | tf_op jit(solution)/shard_map/ppermute | solution.py:369
  15.9 1.9 %collective-permute-start.2 = (bf16[1,128,3584]{2,1,0:T(8,128)(2,1)}, bf16[1,128,3584]{2,1,0:T(8,128)(2,1)}, u32[]{:S(2)}, u32[]{:S(2)}) collective-permute-start(bf16[1,128,3584]{2,1,0:T(8,128)(2,1)} %refs_4_.3), channel_id=1, source_target_pairs={{0,1},{1,0},{2,3},{3,2},{4,5},{5,4},{6,7},{7,6},{8,9},{9,8},{10,11... | collective-permute-start | bytes 2752520 | tf_op jit(solution)/shard_map/ppermute | solution.py:369
  17.8 0.0 collective-permute-done.refs_1_
  17.8 0.0 copy-start.10
  17.9 0.3 collective-permute-done.1.refs_3_
  18.2 0.6 copy-done.10
  18.8 0.0 copy-start.11
  18.8 0.9 copy-done.11
  19.7 0.9 collective-permute-done.2.refs_5_
  20.6 29.4 %all-to-all-done = bf16[16,24,3584]{2,1,0:T(8,128)(2,1)S(1)} async-done(((bf16[16,24,3584]{2,1,0:T(8,128)(2,1)}), bf16[16,24,3584]{2,1,0:T(8,128)(2,1)S(1)}, u32[]{:S(2)}, u32[]{:S(2)}) %all-to-all-start) | async-done | bytes 2752544 | tf_op jit(solution)/shard_map/all_to_all | solution.py:373
  50.1 8.8 %shard_map.132 = (bf16[384,1920]{1,0:T(8,128)(2,1)S(1)}, f32[384,512]{1,0:T(8,128)S(1)}) custom-call(bf16[384,3584]{1,0:T(8,128)(2,1)S(1)} %bitcast.14, bf16[1,3584,128]{2,1,0:T(8,128)(2,1)} %refs_0_.3, bf16[1,3584,128]{2,1,0:T(8,128)(2,1)} %copy-done.10, bf16[1,3584,128]{2,1,0:T(8,128)(2,1)} %refs_2_.3, bf16[1,3584,128]{2,1,0:T(8,128)(2,1)} %copy-done.11, ...), custom_call_target="tpu_custom_call" | custom-call | tf_op jit(solution)/shard_map/pallas_call | solution.py:358
  58.9 0.0 copy-start
  58.9 0.0 copy-start.1
  58.9 0.0 copy-start.2
  58.9 0.0 copy-start.3
  59.0 0.0 copy-start.4
  59.0 0.0 copy-start.7
  59.0 0.0 copy-start.8
  59.0 0.0 copy-start.9
  59.0 25.0 %all_to_all.44 = bf16[16,24,1920]{2,1,0:T(8,128)(2,1)S(1)} all-to-all(bf16[16,24,1920]{2,1,0:T(8,128)(2,1)S(1)} %bitcast.19), channel_id=1, replica_groups=mesh['pipe'=16,'x'=4,'y'=4,'core'=2] {'x','y'}, dimensions={0} | all-to-all | bytes 2949120 | tf_op jit(solution)/shard_map/all_to_all | solution.py:373
  84.0 0.0 copy-start.5
  84.0 0.0 copy-start.6
  84.0 0.0 copy-done
  84.0 0.0 copy-done.1
  84.0 0.0 copy-done.2
  84.0 0.0 copy-done.3
  84.0 0.0 copy-done.4
  84.0 0.0 copy-done.7
  84.0 0.0 copy-done.8
  84.0 0.0 copy-done.9
  84.0 1.0 shard_map.133
  85.0 5.0 %collective-permute-start.3 = (bf16[8,3584]{1,0:T(8,128)(2,1)S(1)}, bf16[8,3584]{1,0:T(8,128)(2,1)S(1)}, u32[]{:S(2)}, u32[]{:S(2)}) collective-permute-start(bf16[8,3584]{1,0:T(8,128)(2,1)S(1)} %get-tuple-element.15.y0_ref), channel_id=1, source_target_pairs={{0,32},{32,64},{64,96},{96,128},{128,160},{160,192},{192,224},{224... | collective-permute-start | bytes 172040 | tf_op jit(solution)/shard_map/ppermute | solution.py:379
  90.1 1.9 %collective-permute-start.4 = (bf16[8,3584]{1,0:T(8,128)(2,1)S(1)}, bf16[8,3584]{1,0:T(8,128)(2,1)S(1)}, u32[]{:S(2)}, u32[]{:S(2)}) collective-permute-start(bf16[8,3584]{1,0:T(8,128)(2,1)S(1)} %get-tuple-element.16.b0_ref), channel_id=1, source_target_pairs={{32,0},{64,32},{96,64},{128,96},{160,128},{192,160},{224,192},{256... | collective-permute-start | bytes 172040 | tf_op jit(solution)/shard_map/ppermute | solution.py:379
  92.0 0.0 collective-permute-done.3.y_ref
  92.0 5.3 %collective-permute-done.4.b_ref = bf16[8,3584]{1,0:T(8,128)(2,1)S(1)} collective-permute-done((bf16[8,3584]{1,0:T(8,128)(2,1)S(1)}, bf16[8,3584]{1,0:T(8,128)(2,1)S(1)}, u32[]{:S(2)}, u32[]{:S(2)}) %collective-permute-start.4) | collective-permute-done | bytes 57376 | tf_op jit(solution)/shard_map/ppermute | solution.py:379
  97.4 0.0 copy-done.5
  97.4 0.0 copy-done.6
  97.4 0.7 shard_map.134
  98.1 19.9 %all_to_all.45 = bf16[16,24,1792]{2,1,0:T(8,128)(2,1)S(1)} all-to-all(bf16[16,24,1792]{2,1,0:T(8,128)(2,1)S(1)} %bitcast.20), channel_id=1, replica_groups=mesh['pipe'=16,'x'=4,'y'=4,'core'=2] {'x','y'}, dimensions={0} | all-to-all | bytes 2752512 | tf_op jit(solution)/shard_map/all_to_all | solution.py:373
  118.1 7.6 %shard_map.135 = bf16[384,1920]{1,0:T(8,128)(2,1)S(1)} custom-call(bf16[384,1792]{1,0:T(8,128)(2,1)S(1)} %bitcast.18, f32[384,512]{1,0:T(8,128)S(1)} %get-tuple-element.18.keep_ref, bf16[1,3584,128]{2,1,0:T(8,128)(2,1)} %refs_0_.3, bf16[1,3584,128]{2,1,0:T(8,128)(2,1)} %copy-done.10, bf16[1,3584,128]{2,1,0:T(8,128)(2,1)} %refs_2_.3, ...), custom_call_target="tpu_custom_call" | custom-call | tf_op jit(solution)/shard_map/pallas_call | solution.py:358
  125.6 19.6 %all_to_all.46 = bf16[16,24,1920]{2,1,0:T(8,128)(2,1)S(1)} all-to-all(bf16[16,24,1920]{2,1,0:T(8,128)(2,1)S(1)} %bitcast.15), channel_id=1, replica_groups=mesh['pipe'=16,'x'=4,'y'=4,'core'=2] {'x','y'}, dimensions={0} | all-to-all | bytes 2949120 | tf_op jit(solution)/shard_map/all_to_all | solution.py:373
  145.2 1.6 %shard_map.136 = (bf16[2,1,8,3584]{3,2,1,0:T(8,128)(2,1)}, bf16[2,1,8,3584]{3,2,1,0:T(8,128)(2,1)}) custom-call(bf16[384,1920]{1,0:T(8,128)(2,1)S(1)} %bitcast.16, bf16[8,3584]{1,0:T(8,128)(2,1)S(1)} %get-tuple-element.19.x_ref, bf16[2,1,8,3584]{3,2,1,0:T(8,128)(2,1)S(1)} %copy-done, bf16[8,3584]{1,0:T(8,128)(2,1)S(1)} %get-tuple-element.20.c_ref, ...), custom_call_target="tpu_custom_call" | custom-call | tf_op jit(solution)/shard_map/pallas_call | solution.py:358
Async XLA Ops:
  4.5 45.6 %all-to-all-start = ((bf16[16,24,3584]{2,1,0:T(8,128)(2,1)}), bf16[16,24,3584]{2,1,0:T(8,128)(2,1)S(1)}, u32[]{:S(2)}, u32[]{:S(2)}) async-start(bf16[16,24,3584]{2,1,0:T(8,128)(2,1)} %bitcast.33), calls=%async_computation | async-start | bytes 5505024 | tf_op jit(solution)/shard_map/all_to_all | solution.py:373
  11.6 6.3 %collective-permute-start = (bf16[1,3584,128]{2,1,0:T(8,128)(2,1)}, bf16[1,3584,128]{2,1,0:T(8,128)(2,1)S(1)}, u32[]{:S(2)}, u32[]{:S(2)}) collective-permute-start(bf16[1,3584,128]{2,1,0:T(8,128)(2,1)} %refs_0_.3), channel_id=1, source_target_pairs={{0,1},{1,0},{2,3},{3,2},{4,5},{5,4},{6,7},{7,6},{8,9},{9,8},{10,11... | collective-permute-start | bytes 2752520 | tf_op jit(solution)/shard_map/ppermute | solution.py:369
  13.5 4.7 %collective-permute-start.1 = (bf16[1,3584,128]{2,1,0:T(8,128)(2,1)}, bf16[1,3584,128]{2,1,0:T(8,128)(2,1)S(1)}, u32[]{:S(2)}, u32[]{:S(2)}) collective-permute-start(bf16[1,3584,128]{2,1,0:T(8,128)(2,1)} %refs_2_.3), channel_id=1, source_target_pairs={{0,1},{1,0},{2,3},{3,2},{4,5},{5,4},{6,7},{7,6},{8,9},{9,8},{10,11... | collective-permute-start | bytes 2752520 | tf_op jit(solution)/shard_map/ppermute | solution.py:369
  15.9 4.7 %collective-permute-start.2 = (bf16[1,128,3584]{2,1,0:T(8,128)(2,1)}, bf16[1,128,3584]{2,1,0:T(8,128)(2,1)}, u32[]{:S(2)}, u32[]{:S(2)}) collective-permute-start(bf16[1,128,3584]{2,1,0:T(8,128)(2,1)} %refs_4_.3), channel_id=1, source_target_pairs={{0,1},{1,0},{2,3},{3,2},{4,5},{5,4},{6,7},{7,6},{8,9},{9,8},{10,11... | collective-permute-start | bytes 2752520 | tf_op jit(solution)/shard_map/ppermute | solution.py:369
  17.8 0.9 copy-start.10
  18.8 0.9 copy-start.11
  58.9 25.1 %copy-start = (bf16[2,1,8,3584]{3,2,1,0:T(8,128)(2,1)S(1)}, bf16[2,1,8,3584]{3,2,1,0:T(8,128)(2,1)}, u32[]{:S(2)}) copy-start(bf16[2,1,8,3584]{3,2,1,0:T(8,128)(2,1)} %s_ref.3) | copy-start | bytes 344068
  58.9 25.1 %copy-start.1 = (bf16[1,3584,4]{1,2,0:T(4,128)(2,1)S(1)}, bf16[1,3584,4]{1,2,0:T(4,128)(2,1)}, u32[]{:S(2)}) copy-start(bf16[1,3584,4]{1,2,0:T(4,128)(2,1)} %param.20) | copy-start | bytes 86020
  58.9 25.0 %copy-start.2 = (bf16[1,8,3584]{2,1,0:T(8,128)(2,1)S(1)}, bf16[1,8,3584]{2,1,0:T(8,128)(2,1)}, u32[]{:S(2)}) copy-start(bf16[1,8,3584]{2,1,0:T(8,128)(2,1)} %x_ref.1) | copy-start | bytes 172036
  58.9 25.0 %copy-start.3 = (bf16[1,8,3584]{2,1,0:T(8,128)(2,1)S(1)}, bf16[1,8,3584]{2,1,0:T(8,128)(2,1)}, u32[]{:S(2)}) copy-start(bf16[1,8,3584]{2,1,0:T(8,128)(2,1)} %c_ref.1) | copy-start | bytes 172036
  59.0 25.0 %copy-start.4 = (bf16[1,3584]{1,0:T(2,128)(2,1)S(1)}, bf16[1,3584]{1,0:T(2,128)(2,1)}, u32[]{:S(2)}) copy-start(bf16[1,3584]{1,0:T(2,128)(2,1)} %gain_ref.5) | copy-start | bytes 21508
  59.0 25.0 %copy-start.7 = (f32[3,8,128]{2,1,0:T(8,128)S(1)}, f32[3,8,128]{2,1,0:T(8,128)}, u32[]{:S(2)}) copy-start(f32[3,8,128]{2,1,0:T(8,128)} %get-tuple-element.14.stat_ref) | copy-start | bytes 36868
  59.0 25.0 %copy-start.8 = (s32[2,1,8,2]{2,3,1,0:T(2,128)S(1)}, s32[2,1,8,2]{2,3,1,0:T(2,128)}, u32[]{:S(2)}) copy-start(s32[2,1,8,2]{2,3,1,0:T(2,128)} %param.17) | copy-start | bytes 388
  59.0 25.0 %copy-start.9 = (s32[2,1,8,2]{2,3,1,0:T(2,128)S(1)}, s32[2,1,8,2]{2,3,1,0:T(2,128)}, u32[]{:S(2)}) copy-start(s32[2,1,8,2]{2,3,1,0:T(2,128)} %param.18) | copy-start | bytes 388
  84.0 13.4 %copy-start.5 = (bf16[1,8,3584]{2,1,0:T(8,128)(2,1)S(1)}, bf16[1,8,3584]{2,1,0:T(8,128)(2,1)}, u32[]{:S(2)}) copy-start(bf16[1,8,3584]{2,1,0:T(8,128)(2,1)} %fnew_ref.1) | copy-start | bytes 172036
  84.0 13.4 %copy-start.6 = (bf16[1,8,3584]{2,1,0:T(8,128)(2,1)S(1)}, bf16[1,8,3584]{2,1,0:T(8,128)(2,1)}, u32[]{:S(2)}) copy-start(bf16[1,8,3584]{2,1,0:T(8,128)(2,1)} %gnew_ref.1) | copy-start | bytes 172036
  85.0 7.0 %collective-permute-start.3 = (bf16[8,3584]{1,0:T(8,128)(2,1)S(1)}, bf16[8,3584]{1,0:T(8,128)(2,1)S(1)}, u32[]{:S(2)}, u32[]{:S(2)}) collective-permute-start(bf16[8,3584]{1,0:T(8,128)(2,1)S(1)} %get-tuple-element.15.y0_ref), channel_id=1, source_target_pairs={{0,32},{32,64},{64,96},{96,128},{128,160},{160,192},{192,224},{224... | collective-permute-start | bytes 172040 | tf_op jit(solution)/shard_map/ppermute | solution.py:379
  90.1 7.3 %collective-permute-start.4 = (bf16[8,3584]{1,0:T(8,128)(2,1)S(1)}, bf16[8,3584]{1,0:T(8,128)(2,1)S(1)}, u32[]{:S(2)}, u32[]{:S(2)}) collective-permute-start(bf16[8,3584]{1,0:T(8,128)(2,1)S(1)} %get-tuple-element.16.b0_ref), channel_id=1, source_target_pairs={{32,0},{64,32},{96,64},{128,96},{160,128},{192,160},{224,192},{256... | collective-permute-start | bytes 172040 | tf_op jit(solution)/shard_map/ppermute | solution.py:379

commit v2 on v1

--- a/solution.py
+++ b/solution.py
@@ -152,111 +152,105 @@
     return pltpu.roll(value, value.shape[0] - count, 0)
 
 
+PAIRS = CHIPS // 2
+SHARED = PAIRS * BLOCK
+
+
+def early_half(width):
+    offset = iota((PAIRS, BLOCK, width), 1)
+    return (offset < 2 * CAP).reshape(SHARED, width), offset.reshape(SHARED, width)
+
+
+def squeezed(value):
+    width = value.shape[1]
+    pairs = value.reshape(PAIRS, 2, BLOCK, width)
+    one, two = (pairs[:, n].reshape(SHARED, width) for n in range(2))
+    return jnp.where(early_half(width)[0], one, pltpu.roll(two, 2 * CAP, 0))
+
+
+def store_halves(out_ref, columns_, left, right):
+    width = left.shape[1]
+    early, _ = early_half(width)
+    one = jnp.where(early, left, pltpu.roll(right, 2 * CAP, 0))
+    two = jnp.where(early, pltpu.roll(left, SHARED - 2 * CAP, 0), right)
+    for n, value in enumerate((one, two)):
+        out_ref[:, n, :, columns_] = value.reshape(PAIRS, BLOCK, width).astype(bf16)
+
+
 def experts(pre, grad_act, gu_ref, down_ref, out_ref):
     hidden = grad_act.shape[1]
-    offset = iota((CHIPS, BLOCK, hidden), 1).reshape(ROWS, hidden)
-    forward = offset < CAP
-    backward = (offset >= CAP) & (offset < 2 * CAP)
+    early, offset = early_half(hidden)
+    forward = jnp.where(early, offset, offset - 2 * CAP) < CAP
     pre_gate, pre_up = pre[:, :hidden], pre[:, hidden:]
     sigma = jax.nn.sigmoid(pre_gate)
     silu = pre_gate * sigma
-    active = silu * pre_up
-    dg = jnp.sum(jnp.where(backward, active.astype(bf16).astype(f32) * grad_act, 0.0), 1, keepdims=True)
+    active = (silu * pre_up).astype(bf16).astype(f32)
+    dg = jnp.sum(jnp.where(forward, 0.0, active * grad_act), 1, keepdims=True)
     grad_up = grad_act * silu
     grad_gate = grad_act * pre_up * sigma * (1.0 + pre_gate * (1.0 - sigma))
-    parts = [
-        jnp.where(forward, active, 0.0),
-        jnp.where(backward, grad_gate, 0.0),
-        jnp.where(backward, grad_up, 0.0),
-    ]
-    parts = [(p + pltpu.roll(p, 2 * CAP, 0)).astype(bf16) for p in parts]
-    grads = jnp.concatenate(parts[1:], 1)
+    active = jnp.where(forward, active, 0.0).astype(bf16)
+    grads = jnp.concatenate([jnp.where(forward, 0.0, grad_gate), jnp.where(forward, 0.0, grad_up)], 1).astype(bf16)
     width = down_ref.shape[1] // 2
     step = 256
-    left = iota((CHIPS, BLOCK, step), 1).reshape(ROWS, step) < 2 * CAP
     for n in range(0, width, step):
         sides = []
         for at in (n, n + width):
-            side = dot(parts[0], down_ref[:, at : at + step])
-            sides.append(side + dot_nt(grads, gu_ref[at : at + step, :]))
-        out_ref[:, n : n + step] = jnp.where(left, sides[0], sides[1]).astype(bf16)
+            side = dot(active, down_ref[:, at : at + step])
+            sides.append(side + dot(grads, gu_ref[:, at : at + step]))
+        store_halves(out_ref, pl.ds(n, step), *sides)
     high = dg.astype(bf16).astype(f32)
-    low = pltpu.roll(jnp.broadcast_to(dg - high, (ROWS, PACK)), 2 * CAP, 0)
-    high = jnp.broadcast_to(high, (ROWS, PACK))
-    out_ref[:, width : width + PACK] = jnp.where(left[:, :PACK], high, low).astype(bf16)
+    pair = [jnp.broadcast_to(v, (SHARED, PACK)) for v in (high, dg - high)]
+    store_halves(out_ref, pl.ds(width, PACK), *pair)
 
 
 CHUNKS = 4
 
 
 class Weights:
-    def __init__(self, w_hbm, gu_ref, down_ref, sems):
-        depth, width = w_hbm[0].shape[1:]
-        self.chunk = depth // CHUNKS
-        self.groups = []
-        for n in range(CHUNKS):
-            at = pl.ds(n * self.chunk, self.chunk)
-            self.groups.append(
-                [
-                    pltpu.make_async_copy(
-                        w_hbm[i].at[0, at, :], gu_ref.at[at, i * width : (i + 1) * width], sems.at[n * 4 + i]
-                    )
-                    for i in range(4)
-                ]
-            )
-        self.groups.append(
-            [
-                pltpu.make_async_copy(
-                    w_hbm[4 + i].at[0], down_ref.at[i * width : (i + 1) * width, :], sems.at[CHUNKS * 4 + i]
-                )
-                for i in range(2)
-            ]
-        )
-        self.start(0)
-        self.start(1)
-
-    def start(self, n):
-        if n < len(self.groups):
-            for copy in self.groups[n]:
-                copy.start()
+    def __init__(self, gu_hbm, down_hbm, gu_ref, down_ref, sems):
+        self.chunk = gu_hbm.shape[1] // CHUNKS
+        at = [pl.ds(n * self.chunk, self.chunk) for n in range(CHUNKS)]
+        self.copies = [
+            pltpu.make_async_copy(gu_hbm.at[:, a], gu_ref.at[:, a], sems.at[n]) for n, a in enumerate(at)
+        ]
+        self.copies.append(pltpu.make_async_copy(down_hbm, down_ref, sems.at[CHUNKS]))
+        for copy in self.copies:
+            copy.start()
 
     def wait(self, n):
-        for copy in self.groups[n]:
-            copy.wait()
-        self.start(n + 2)
-
-
-def experts_first_kernel(in_ref, *refs):
-    w_hbm, (out_ref, keep_ref, gu_ref, down_ref, sems) = refs[:6], refs[6:]
-    weights = Weights(w_hbm, gu_ref, down_ref, sems)
+        self.copies[n].wait()
+
+
+def experts_first_kernel(in_ref, gu_hbm, down_hbm, out_ref, keep_ref, gu_ref, down_ref, sems):
+    weights = Weights(gu_hbm, down_hbm, gu_ref, down_ref, sems)
     pre = 0.0
     for n in range(CHUNKS):
         weights.wait(n)
         at = slice(n * weights.chunk, (n + 1) * weights.chunk)
-        pre = pre + dot(in_ref[:, at], gu_ref[at, :])
-    keep_ref[...] = roll_up(pre, 2 * CAP)
+        pre = pre + dot_nt(in_ref[:, at], gu_ref[:, at])
+    keep_ref[...] = squeezed(roll_up(pre, 2 * CAP))
     weights.wait(CHUNKS)
-    grad_act = roll_up(dot_nt(in_ref[...], down_ref[...]), CAP)
-    experts(pre, grad_act, gu_ref, down_ref, out_ref)
-
-
-def experts_second_kernel(in_ref, keep_ref, *refs):
-    w_hbm, (out_ref, gu_ref, down_ref, sems) = refs[:6], refs[6:]
-    weights = Weights(w_hbm, gu_ref, down_ref, sems)
+    grad_act = squeezed(roll_up(dot_nt(in_ref[...], down_ref[...]), CAP))
+    experts(squeezed(pre), grad_act, gu_ref, down_ref, out_ref)
+
+
+def experts_second_kernel(in_ref, keep_ref, gu_hbm, down_hbm, out_ref, gu_ref, down_ref, sems):
+    weights = Weights(gu_hbm, down_hbm, gu_ref, down_ref, sems)
     width = in_ref.shape[1]
     sides = [0.0, 0.0]
     for n in range(CHUNKS):
         weights.wait(n)
         h, at = divmod(n * weights.chunk, width)
-        part = dot(in_ref[:, at : at + weights.chunk], gu_ref[n * weights.chunk : (n + 1) * weights.chunk, :])
+        part = dot_nt(in_ref[:, at : at + weights.chunk], gu_ref[:, n * weights.chunk : (n + 1) * weights.chunk])
         sides[h] = sides[h] + part
-    pre = sides[0] + roll_up(sides[1], 2 * CAP)
+    pre = squeezed(sides[0] + roll_up(sides[1], 2 * CAP))
     weights.wait(CHUNKS)
     rows = in_ref[...]
     grad_act = dot_nt(rows, down_ref[:, :width]) + roll_up(dot_nt(rows, down_ref[:, width:]), 2 * CAP)
-    offset = iota((CHIPS, BLOCK, pre.shape[1]), 1).reshape(pre.shape)
-    pre = jnp.where(offset < CAP, pre, keep_ref[...])
-    experts(pre, grad_act, gu_ref, down_ref, out_ref)
+    early, offset = early_half(pre.shape[1])
+    forward = jnp.where(early, offset, offset - 2 * CAP) < CAP
+    pre = jnp.where(forward, pre, keep_ref[...])
+    experts(pre, squeezed(grad_act), gu_ref, down_ref, out_ref)
 
 
 def combine(in_ref, x, s, cot, x_stat, s_stat, fid, bid, gain, router_rows):
@@ -349,12 +343,8 @@
     outs = [jax.ShapeDtypeStruct(*o) for o in outs]
     scratch = []
     if weights:
-        depth, width = weights[0].shape[1:]
-        scratch = [
-            pltpu.VMEM((depth, 4 * width), bf16),
-            pltpu.VMEM((2 * width, depth), bf16),
-            pltpu.SemaphoreType.DMA((CHUNKS * 4 + 2,)),
-        ]
+        scratch = [pltpu.VMEM(w.shape, w.dtype) for w in weights]
+        scratch.append(pltpu.SemaphoreType.DMA((CHUNKS + 1,)))
     return pl.pallas_call(
         kernel,
         out_shape=outs,
@@ -370,6 +360,7 @@
 
 
 def exchanged(block):
+    block = block.reshape(ROWS, block.shape[-1])
     return lax.all_to_all(block, ("x", "y"), split_axis=0, concat_axis=0, tiled=True)
 
 
@@ -403,15 +394,17 @@
         ],
         compiler_params=pltpu.CompilerParams(vmem_limit_bytes=PREPARE_BYTES),
     )(*in_hbm(args))
-    weights = []
-    for own in (gate_proj, up_proj, down_proj):
-        weights += [own, swapped(own)]
-    hidden = 4 * gate_proj.shape[-1]
-    packed = (ROWS, width // 2 + PACK)
+    gates_, ups, downs = gate_proj[0], up_proj[0], down_proj[0]
+    weights = (
+        jnp.concatenate([w.T for w in (gates_, swapped(gates_), ups, swapped(ups))], 0),
+        jnp.concatenate([downs, swapped(downs)], 0),
+    )
+    hidden = weights[0].shape[0]
+    packed = (PAIRS, 2, BLOCK, width // 2 + PACK)
 
     came = exchanged(sent)
     sent, keep = call(
-        experts_first_kernel, [(packed, bf16), ((ROWS, hidden), f32)], came, weights=weights
+        experts_first_kernel, [(packed, bf16), ((SHARED, hidden), f32)], came, weights=weights
     )
     came = exchanged(sent)
     y0, b0 = call(

time: 147 us -> 144 us (0.980)
  waiting for transfers between devices: 36 us -> 27.1 us
  other arithmetic: 0 us -> 5.83 us
  Pallas kernels: 23.6 us -> 20.3 us
  local copies, waits for them, and re-layouts: 1.57 us -> 4.61 us
    all_to_all x1, waiting for transfers between devices: 29.4 us -> 21.7 us  [exchanged(): lax.all_to_all(block, ('x', 'y'), split_axis=0, concat_axis=0, tiled=True)]
    concatenate x0 -> x2, other arithmetic: none -> 5.83 us  [the longest x1 2.99 us: per_device(): jnp.concatenate([w.T for w in (gates_, swapped(gates_), ups, swapped(ups)...]
    pallas_call x5, Pallas kernels: 19.8 us -> 16.4 us  [call(): pl.pallas_call(kernel, out_shape=outs, in_specs=[first] * smem + [spec] *...]
    unnamed x24 -> x26, local copies, waits for them, and re-layouts: 1.57 us -> 4.61 us
  transfers between devices with their start and end apart: 6 -> 6, of which waited for: 4 -> 2; matrix products, arithmetic and copies ran while one was open for 0% -> 7% of each run, Pallas kernels for 0% -> 0%
where the time goes in v2:
time: 144 us; the launch traced here: 143 us
  blocking collectives  64.5 us (45%)
  waiting for transfers between devices  27.1 us (19%)
  starting transfers between devices  20.4 us (14%)
  Pallas kernels  20.3 us (14%)
  other arithmetic  5.83 us (4%)
  local copies, waits for them, and re-layouts  4.61 us (3%)
    all_to_all x3, blocking collectives, exchanged(): lax.all_to_all(block, ('x', 'y'), split_axis=0, concat_axis=0, tiled=True)  64.5 us
    all_to_all x1, waiting for transfers between devices, exchanged(): lax.all_to_all(block, ('x', 'y'), split_axis=0, concat_axis=0, tiled=True)  21.7 us
    pallas_call x5, Pallas kernels, call(): pl.pallas_call(kernel, out_shape=outs, in_specs=[first] * smem + [spec] *...  16.4 us
    all_to_all x1, starting transfers between devices, exchanged(): lax.all_to_all(block, ('x', 'y'), split_axis=0, concat_axis=0, tiled=True)  7.05 us
    ppermute x2, starting transfers between devices, shifted(): return lax.ppermute(block, 'pipe', route_)  6.95 us
    ppermute x3, starting transfers between devices, swapped(): return lax.ppermute(block, 'core', [(0, 1), (1, 0)])  6.36 us
    ppermute x2, waiting for transfers between devices, shifted(): return lax.ppermute(block, 'pipe', route_)  5.34 us
    unnamed x26, local copies, waits for them, and re-layouts  4.61 us
  transfers between devices with their start and end apart: 6, of which 2 were waited for; matrix products, arithmetic and copies ran while one was open for 7% of the time, Pallas kernels for 0%

profile of v2, /device:TPU:224, one launch (start us, length us, event | category | flops | bytes accessed | tf_op | source)
XLA Modules:
  0.0 143.5 jit_solution(17166486268438924582)
XLA Ops:
  0.6 3.9 %shard_map.131 = (bf16[384,3584]{1,0:T(8,128)(2,1)}, f32[3,8,128]{2,1,0:T(8,128)}) custom-call(bf16[1,8,3584]{2,1,0:T(8,128)(2,1)} %x_ref.1, bf16[2,1,8,3584]{3,2,1,0:T(8,128)(2,1)} %s_ref.3, bf16[1,8,3584]{2,1,0:T(8,128)(2,1)} %c_ref.1, bf16[1,3584]{1,0:T(2,128)(2,1)} %gain_ref.5, bf16[4,3584]{1,0:T(4,128)(2,1)} %bitcast.30, s32[2,1,2,8]{3,2,1,0:T(2,128)} %bitcast.34, ...), custom_call_target="tpu_custom_call" | custom-call | tf_op jit(solution)/shard_map/pallas_call | solution.py:384
  4.5 7.0 %all-to-all-start = ((bf16[16,24,3584]{2,1,0:T(8,128)(2,1)}), bf16[16,24,3584]{2,1,0:T(8,128)(2,1)S(1)}, u32[]{:S(2)}, u32[]{:S(2)}) async-start(bf16[16,24,3584]{2,1,0:T(8,128)(2,1)} %bitcast.46), calls=%async_computation | async-start | bytes 5505024 | tf_op jit(solution)/shard_map/all_to_all | solution.py:364
  11.6 1.9 %collective-permute-start.2 = (bf16[128,3584]{1,0:T(8,128)(2,1)}, bf16[128,3584]{1,0:T(8,128)(2,1)}, u32[]{:S(2)}, u32[]{:S(2)}) collective-permute-start(bf16[128,3584]{1,0:T(8,128)(2,1)} %bitcast.47), channel_id=1, source_target_pairs={{0,1},{1,0},{2,3},{3,2},{4,5},{5,4},{6,7},{7,6},{8,9},{9,8},{10,11... | collective-permute-start | bytes 2752520 | tf_op jit(solution)/shard_map/ppermute | solution.py:359
  13.5 2.3 %copy.15 = bf16[1,3584,128]{1,2,0:T(8,128)(2,1)} copy(bf16[1,3584,128]{2,1,0:T(8,128)(2,1)} %param.22) | data formatting | bytes 1835008 | tf_op args[10]
  15.8 2.4 %collective-permute-start.1 = (bf16[3584,128]{0,1:T(8,128)(2,1)}, bf16[3584,128]{0,1:T(8,128)(2,1)}, u32[]{:S(2)}, u32[]{:S(2)}) collective-permute-start(bf16[3584,128]{0,1:T(8,128)(2,1)} %bitcast.42), channel_id=1, source_target_pairs={{0,1},{1,0},{2,3},{3,2},{4,5},{5,4},{6,7},{7,6},{8,9},{9,8},{10,11... | collective-permute-start | bytes 2752520 | tf_op jit(solution)/shard_map/ppermute | solution.py:359
  18.2 2.3 %copy.14 = bf16[1,3584,128]{1,2,0:T(8,128)(2,1)} copy(bf16[1,3584,128]{2,1,0:T(8,128)(2,1)} %param.21) | data formatting | bytes 1835008 | tf_op args[9]
  20.4 0.0 copy-start.11
  20.4 2.0 %collective-permute-start = (bf16[3584,128]{0,1:T(8,128)(2,1)}, bf16[3584,128]{0,1:T(8,128)(2,1)S(1)}, u32[]{:S(2)}, u32[]{:S(2)}) collective-permute-start(bf16[3584,128]{0,1:T(8,128)(2,1)} %bitcast.44), channel_id=1, source_target_pairs={{0,1},{1,0},{2,3},{3,2},{4,5},{5,4},{6,7},{7,6},{8,9},{9,8},{10,11... | collective-permute-start | bytes 2752520 | tf_op jit(solution)/shard_map/ppermute | solution.py:359
  22.5 0.0 collective-permute-done.2
  22.5 2.8 %pad_maximum_fusion.1.down_hbm = bf16[256,3584]{1,0:T(8,128)(2,1)} fusion(bf16[128,3584]{1,0:T(8,128)(2,1)} %collective-permute-done.2, bf16[128,3584]{1,0:T(8,128)(2,1)} %bitcast.48), kind=kLoop, calls=%fused_computation.1 | loop fusion | flops 3670016 | bytes 3670016 | tf_op jit(solution)/shard_map/concatenate | solution.py:400
  25.3 0.0 collective-permute-done.1
  25.3 0.0 collective-permute-done
  25.3 0.0 copy-done.10
  25.4 0.0 copy-done.11
  25.4 3.0 %pad_maximum_fusion.gu_hbm = bf16[512,3584]{1,0:T(8,128)(2,1)} fusion(bf16[128,3584]{1,0:T(8,128)(2,1)} %bitcast.12, bf16[128,3584]{1,0:T(8,128)(2,1)S(1)} %bitcast.43, bf16[128,3584]{1,0:T(8,128)(2,1)S(1)} %bitcast.49, bf16[128,3584]{1,0:T(8,128)(2,1)S(1)} %bitcast.45), kind=kLoop, calls=%fused_computation | loop fusion | flops 14680064 | bytes 7340032 | tf_op jit(solution)/shard_map/concatenate | solution.py:399
  28.4 21.7 %all-to-all-done = bf16[16,24,3584]{2,1,0:T(8,128)(2,1)S(1)} async-done(((bf16[16,24,3584]{2,1,0:T(8,128)(2,1)}), bf16[16,24,3584]{2,1,0:T(8,128)(2,1)S(1)}, u32[]{:S(2)}, u32[]{:S(2)}) %all-to-all-start) | async-done | bytes 2752544 | tf_op jit(solution)/shard_map/all_to_all | solution.py:364
  50.1 0.0 copy-start
  50.1 0.0 copy-start.1
  50.1 0.0 copy-start.2
  50.1 0.0 copy-start.3
  50.1 0.0 copy-start.4
  50.1 0.0 copy-start.7
  50.1 0.0 copy-start.8
  50.1 0.0 copy-start.9
  50.1 7.2 %shard_map.132 = (bf16[8,2,24,1920]{3,2,1,0:T(8,128)(2,1)S(1)}, f32[192,512]{1,0:T(8,128)S(1)}) custom-call(bf16[384,3584]{1,0:T(8,128)(2,1)S(1)} %bitcast.23, bf16[512,3584]{1,0:T(8,128)(2,1)} %pad_maximum_fusion.gu_hbm, bf16[256,3584]{1,0:T(8,128)(2,1)} %pad_maximum_fusion.1.down_hbm), custom_call_target="tpu_custom_call" | custom-call | tf_op jit(solution)/shard_map/pallas_call | solution.py:348
  57.3 0.0 copy-start.5
  57.3 0.0 copy-start.6
  57.4 24.9 %all_to_all.44 = bf16[16,24,1920]{2,1,0:T(8,128)(2,1)S(1)} all-to-all(bf16[16,24,1920]{2,1,0:T(8,128)(2,1)S(1)} %bitcast.28), channel_id=1, replica_groups=mesh['pipe'=16,'x'=4,'y'=4,'core'=2] {'x','y'}, dimensions={0} | all-to-all | bytes 2949120 | tf_op jit(solution)/shard_map/all_to_all | solution.py:364
  82.3 0.0 copy-done
  82.3 0.0 copy-done.1
  82.3 0.0 copy-done.2
  82.3 0.0 copy-done.3
  82.3 0.0 copy-done.4
  82.3 0.0 copy-done.7
  82.3 0.0 copy-done.8
  82.3 0.0 copy-done.9
  82.4 1.0 shard_map.133
  83.4 5.0 %collective-permute-start.3 = (bf16[8,3584]{1,0:T(8,128)(2,1)S(1)}, bf16[8,3584]{1,0:T(8,128)(2,1)S(1)}, u32[]{:S(2)}, u32[]{:S(2)}) collective-permute-start(bf16[8,3584]{1,0:T(8,128)(2,1)S(1)} %get-tuple-element.15.y0_ref), channel_id=1, source_target_pairs={{0,32},{32,64},{64,96},{96,128},{128,160},{160,192},{192,224},{224... | collective-permute-start | bytes 172040 | tf_op jit(solution)/shard_map/ppermute | solution.py:370
  88.4 1.9 %collective-permute-start.4 = (bf16[8,3584]{1,0:T(8,128)(2,1)S(1)}, bf16[8,3584]{1,0:T(8,128)(2,1)S(1)}, u32[]{:S(2)}, u32[]{:S(2)}) collective-permute-start(bf16[8,3584]{1,0:T(8,128)(2,1)S(1)} %get-tuple-element.16.b0_ref), channel_id=1, source_target_pairs={{32,0},{64,32},{96,64},{128,96},{160,128},{192,160},{224,192},{256... | collective-permute-start | bytes 172040 | tf_op jit(solution)/shard_map/ppermute | solution.py:370
  90.3 0.0 collective-permute-done.3.y_ref
  90.3 5.3 %collective-permute-done.4.b_ref = bf16[8,3584]{1,0:T(8,128)(2,1)S(1)} collective-permute-done((bf16[8,3584]{1,0:T(8,128)(2,1)S(1)}, bf16[8,3584]{1,0:T(8,128)(2,1)S(1)}, u32[]{:S(2)}, u32[]{:S(2)}) %collective-permute-start.4) | collective-permute-done | bytes 57376 | tf_op jit(solution)/shard_map/ppermute | solution.py:370
  95.7 0.0 copy-done.5
  95.7 0.0 copy-done.6
  95.7 0.7 shard_map.134
  96.4 19.9 %all_to_all.45 = bf16[16,24,1792]{2,1,0:T(8,128)(2,1)S(1)} all-to-all(bf16[16,24,1792]{2,1,0:T(8,128)(2,1)S(1)} %bitcast.29), channel_id=1, replica_groups=mesh['pipe'=16,'x'=4,'y'=4,'core'=2] {'x','y'}, dimensions={0} | all-to-all | bytes 2752512 | tf_op jit(solution)/shard_map/all_to_all | solution.py:364
  116.4 5.9 %shard_map.135 = bf16[8,2,24,1920]{3,2,1,0:T(8,128)(2,1)S(1)} custom-call(bf16[384,1792]{1,0:T(8,128)(2,1)S(1)} %bitcast.27, f32[192,512]{1,0:T(8,128)S(1)} %get-tuple-element.18.keep_ref, bf16[512,3584]{1,0:T(8,128)(2,1)} %pad_maximum_fusion.gu_hbm, bf16[256,3584]{1,0:T(8,128)(2,1)} %pad_maximum_fusion.1.down_hbm), custom_call_target="tpu_custom_call" | custom-call | tf_op jit(solution)/shard_map/pallas_call | solution.py:348
  122.3 19.6 %all_to_all.46 = bf16[16,24,1920]{2,1,0:T(8,128)(2,1)S(1)} all-to-all(bf16[16,24,1920]{2,1,0:T(8,128)(2,1)S(1)} %bitcast.26), channel_id=1, replica_groups=mesh['pipe'=16,'x'=4,'y'=4,'core'=2] {'x','y'}, dimensions={0} | all-to-all | bytes 2949120 | tf_op jit(solution)/shard_map/all_to_all | solution.py:364
  141.8 1.6 %shard_map.136 = (bf16[2,1,8,3584]{3,2,1,0:T(8,128)(2,1)}, bf16[2,1,8,3584]{3,2,1,0:T(8,128)(2,1)}) custom-call(bf16[384,1920]{1,0:T(8,128)(2,1)S(1)} %bitcast.24, bf16[8,3584]{1,0:T(8,128)(2,1)S(1)} %get-tuple-element.19.x_ref, bf16[2,1,8,3584]{3,2,1,0:T(8,128)(2,1)S(1)} %copy-done, bf16[8,3584]{1,0:T(8,128)(2,1)S(1)} %get-tuple-element.20.c_ref, ...), custom_call_target="tpu_custom_call" | custom-call | tf_op jit(solution)/shard_map/pallas_call | solution.py:348
  (1 shorter events, 0.0 us)
Async XLA Ops:
  4.5 45.6 %all-to-all-start = ((bf16[16,24,3584]{2,1,0:T(8,128)(2,1)}), bf16[16,24,3584]{2,1,0:T(8,128)(2,1)S(1)}, u32[]{:S(2)}, u32[]{:S(2)}) async-start(bf16[16,24,3584]{2,1,0:T(8,128)(2,1)} %bitcast.46), calls=%async_computation | async-start | bytes 5505024 | tf_op jit(solution)/shard_map/all_to_all | solution.py:364
  11.6 10.9 %collective-permute-start.2 = (bf16[128,3584]{1,0:T(8,128)(2,1)}, bf16[128,3584]{1,0:T(8,128)(2,1)}, u32[]{:S(2)}, u32[]{:S(2)}) collective-permute-start(bf16[128,3584]{1,0:T(8,128)(2,1)} %bitcast.47), channel_id=1, source_target_pairs={{0,1},{1,0},{2,3},{3,2},{4,5},{5,4},{6,7},{7,6},{8,9},{9,8},{10,11... | collective-permute-start | bytes 2752520 | tf_op jit(solution)/shard_map/ppermute | solution.py:359
  15.8 9.6 %collective-permute-start.1 = (bf16[3584,128]{0,1:T(8,128)(2,1)}, bf16[3584,128]{0,1:T(8,128)(2,1)}, u32[]{:S(2)}, u32[]{:S(2)}) collective-permute-start(bf16[3584,128]{0,1:T(8,128)(2,1)} %bitcast.42), channel_id=1, source_target_pairs={{0,1},{1,0},{2,3},{3,2},{4,5},{5,4},{6,7},{7,6},{8,9},{9,8},{10,11... | collective-permute-start | bytes 2752520 | tf_op jit(solution)/shard_map/ppermute | solution.py:359
  20.4 4.9 %copy-start.10 = (bf16[1,3584,128]{1,2,0:T(8,128)(2,1)S(1)}, bf16[1,3584,128]{1,2,0:T(8,128)(2,1)}, u32[]{:S(2)}) copy-start(bf16[1,3584,128]{1,2,0:T(8,128)(2,1)} %copy.15) | copy-start | bytes 2752516
  20.4 4.9 %copy-start.11 = (bf16[1,3584,128]{1,2,0:T(8,128)(2,1)S(1)}, bf16[1,3584,128]{1,2,0:T(8,128)(2,1)}, u32[]{:S(2)}) copy-start(bf16[1,3584,128]{1,2,0:T(8,128)(2,1)} %copy.14) | copy-start | bytes 2752516
  20.4 4.9 %collective-permute-start = (bf16[3584,128]{0,1:T(8,128)(2,1)}, bf16[3584,128]{0,1:T(8,128)(2,1)S(1)}, u32[]{:S(2)}, u32[]{:S(2)}) collective-permute-start(bf16[3584,128]{0,1:T(8,128)(2,1)} %bitcast.44), channel_id=1, source_target_pairs={{0,1},{1,0},{2,3},{3,2},{4,5},{5,4},{6,7},{7,6},{8,9},{9,8},{10,11... | collective-permute-start | bytes 2752520 | tf_op jit(solution)/shard_map/ppermute | solution.py:359
  50.1 32.2 %copy-start = (bf16[2,1,8,3584]{3,2,1,0:T(8,128)(2,1)S(1)}, bf16[2,1,8,3584]{3,2,1,0:T(8,128)(2,1)}, u32[]{:S(2)}) copy-start(bf16[2,1,8,3584]{3,2,1,0:T(8,128)(2,1)} %s_ref.3) | copy-start | bytes 344068
  50.1 32.2 %copy-start.1 = (bf16[1,3584,4]{1,2,0:T(4,128)(2,1)S(1)}, bf16[1,3584,4]{1,2,0:T(4,128)(2,1)}, u32[]{:S(2)}) copy-start(bf16[1,3584,4]{1,2,0:T(4,128)(2,1)} %param.20) | copy-start | bytes 86020
  50.1 32.2 %copy-start.2 = (bf16[1,8,3584]{2,1,0:T(8,128)(2,1)S(1)}, bf16[1,8,3584]{2,1,0:T(8,128)(2,1)}, u32[]{:S(2)}) copy-start(bf16[1,8,3584]{2,1,0:T(8,128)(2,1)} %x_ref.1) | copy-start | bytes 172036
  50.1 32.2 %copy-start.3 = (bf16[1,8,3584]{2,1,0:T(8,128)(2,1)S(1)}, bf16[1,8,3584]{2,1,0:T(8,128)(2,1)}, u32[]{:S(2)}) copy-start(bf16[1,8,3584]{2,1,0:T(8,128)(2,1)} %c_ref.1) | copy-start | bytes 172036
  50.1 32.2 %copy-start.4 = (bf16[1,3584]{1,0:T(2,128)(2,1)S(1)}, bf16[1,3584]{1,0:T(2,128)(2,1)}, u32[]{:S(2)}) copy-start(bf16[1,3584]{1,0:T(2,128)(2,1)} %gain_ref.5) | copy-start | bytes 21508
  50.1 32.2 %copy-start.7 = (f32[3,8,128]{2,1,0:T(8,128)S(1)}, f32[3,8,128]{2,1,0:T(8,128)}, u32[]{:S(2)}) copy-start(f32[3,8,128]{2,1,0:T(8,128)} %get-tuple-element.14.stat_ref) | copy-start | bytes 36868
  50.1 32.2 %copy-start.8 = (s32[2,1,8,2]{2,3,1,0:T(2,128)S(1)}, s32[2,1,8,2]{2,3,1,0:T(2,128)}, u32[]{:S(2)}) copy-start(s32[2,1,8,2]{2,3,1,0:T(2,128)} %param.17) | copy-start | bytes 388
  50.1 32.2 %copy-start.9 = (s32[2,1,8,2]{2,3,1,0:T(2,128)S(1)}, s32[2,1,8,2]{2,3,1,0:T(2,128)}, u32[]{:S(2)}) copy-start(s32[2,1,8,2]{2,3,1,0:T(2,128)} %param.18) | copy-start | bytes 388
  57.3 38.3 %copy-start.5 = (bf16[1,8,3584]{2,1,0:T(8,128)(2,1)S(1)}, bf16[1,8,3584]{2,1,0:T(8,128)(2,1)}, u32[]{:S(2)}) copy-start(bf16[1,8,3584]{2,1,0:T(8,128)(2,1)} %fnew_ref.1) | copy-start | bytes 172036
  57.3 38.3 %copy-start.6 = (bf16[1,8,3584]{2,1,0:T(8,128)(2,1)S(1)}, bf16[1,8,3584]{2,1,0:T(8,128)(2,1)}, u32[]{:S(2)}) copy-start(bf16[1,8,3584]{2,1,0:T(8,128)(2,1)} %gnew_ref.1) | copy-start | bytes 172036
  83.4 7.0 %collective-permute-start.3 = (bf16[8,3584]{1,0:T(8,128)(2,1)S(1)}, bf16[8,3584]{1,0:T(8,128)(2,1)S(1)}, u32[]{:S(2)}, u32[]{:S(2)}) collective-permute-start(bf16[8,3584]{1,0:T(8,128)(2,1)S(1)} %get-tuple-element.15.y0_ref), channel_id=1, source_target_pairs={{0,32},{32,64},{64,96},{96,128},{128,160},{160,192},{192,224},{224... | collective-permute-start | bytes 172040 | tf_op jit(solution)/shard_map/ppermute | solution.py:370
  88.4 7.3 %collective-permute-start.4 = (bf16[8,3584]{1,0:T(8,128)(2,1)S(1)}, bf16[8,3584]{1,0:T(8,128)(2,1)S(1)}, u32[]{:S(2)}, u32[]{:S(2)}) collective-permute-start(bf16[8,3584]{1,0:T(8,128)(2,1)S(1)} %get-tuple-element.16.b0_ref), channel_id=1, source_target_pairs={{32,0},{64,32},{96,64},{128,96},{160,128},{192,160},{224,192},{256... | collective-permute-start | bytes 172040 | tf_op jit(solution)/shard_map/ppermute | solution.py:370

commit v3 on v2

--- a/solution.py
+++ b/solution.py
@@ -96,9 +96,36 @@
     return jnp.where(at == 0, affin[0], jnp.where(at == 1, affin[1], inverse))
 
 
+def turned(g_hbm, u_hbm, out_hbm, w_ref, t_ref, sem):
+    reads = [pltpu.make_async_copy(w, w_ref.at[n], sem.at[n]) for n, w in enumerate((g_hbm, u_hbm))]
+    for read in reads:
+        read.start()
+    depth, width = w_ref.shape[-2:]
+    writes = []
+    for n, read in enumerate(reads):
+        read.wait()
+        rows = pl.ds(n * width, width)
+        for at in range(0, depth, 128):
+            t_ref[rows, at : at + 128] = w_ref[n, 0, at : at + 128, :].T
+        writes.append(pltpu.make_async_copy(t_ref.at[rows], out_hbm.at[rows], sem.at[2 + n]))
+        writes[-1].start()
+    for write in writes:
+        write.wait()
+
+
+def turn_kernel(core_ref, before_hbm, g_hbm, u_hbm, out_hbm, w_ref, t_ref, sem):
+    del before_hbm
+
+    @pl.when(core_ref[0, 0] == 0)
+    def _():
+        turned(g_hbm, u_hbm, out_hbm, w_ref, t_ref, sem)
+
+
 def prepare_kernel(
-    x_hbm, s_hbm, c_hbm, gain_hbm, router_hbm, fid_hbm, bid_hbm, out_hbm, stat_ref,
+    core_ref, x_hbm, s_hbm, c_hbm, gain_hbm, router_hbm, fid_hbm, bid_hbm, g_hbm, u_hbm,
+    out_hbm, stat_ref, turned_hbm,
     x_ref, s_ref, c_ref, gain_ref, router_ref, fid_ref, bid_ref, out_ref, in_sem, out_sem,
+    w_ref, t_ref, w_sem,
 ):
     sources = (fid_hbm, bid_hbm, x_hbm, s_hbm, gain_hbm, router_hbm, c_hbm)
     places = (fid_ref, bid_ref, x_ref, s_ref, gain_ref, router_ref, c_ref)
@@ -125,6 +152,11 @@
         out_ref[at] = dot(table[e * step : (e + 1) * step].astype(bf16), stacked).astype(bf16)
         sends.append(pltpu.make_async_copy(out_ref.at[at], out_hbm.at[at], out_sem.at[e]))
         sends[-1].start()
+
+    @pl.when(core_ref[0, 0] == 1)
+    def _():
+        turned(g_hbm, u_hbm, turned_hbm, w_ref, t_ref, w_sem)
+
     for send in sends:
         send.wait()
 
@@ -381,28 +413,51 @@
     backward_ids = backward_ids.transpose(0, 1, 3, 2)
     router = router[0].T
     args = (forward_in, saved_inputs, grad_in, norm_gain, router, forward_ids, backward_ids)
-    sent, stats = pl.pallas_call(
+    core = lax.axis_index("core").astype(jnp.int32).reshape(1, 1)
+    shard = gate_proj.shape[-1]
+    turn_scratch = [
+        pltpu.VMEM((2, *gate_proj.shape), bf16),
+        pltpu.VMEM((2 * shard, width), bf16),
+        pltpu.SemaphoreType.DMA((4,)),
+    ]
+    smem = pl.BlockSpec(memory_space=pltpu.SMEM)
+    far = pl.BlockSpec(memory_space=pltpu.HBM)
+    rows_of = jax.ShapeDtypeStruct((2 * shard, width), bf16)
+    sent, stats, rows_ = pl.pallas_call(
         prepare_kernel,
-        out_shape=[jax.ShapeDtypeStruct((ROWS, width), bf16), jax.ShapeDtypeStruct((3, *stat), f32)],
-        in_specs=[pl.BlockSpec(memory_space=pltpu.HBM)] * len(args),
-        out_specs=[pl.BlockSpec(memory_space=pltpu.HBM), pl.BlockSpec(memory_space=pltpu.VMEM)],
+        out_shape=[
+            jax.ShapeDtypeStruct((ROWS, width), bf16), jax.ShapeDtypeStruct((3, *stat), f32), rows_of
+        ],
+        in_specs=[smem] + [far] * (len(args) + 2),
+        out_specs=[far, pl.BlockSpec(memory_space=pltpu.VMEM), far],
         scratch_shapes=[pltpu.VMEM(a.shape, a.dtype) for a in args]
         + [
             pltpu.VMEM((ROWS, width), bf16),
             pltpu.SemaphoreType.DMA((len(args),)),
             pltpu.SemaphoreType.DMA((EXPERTS,)),
-        ],
+        ]
+        + turn_scratch,
         compiler_params=pltpu.CompilerParams(vmem_limit_bytes=PREPARE_BYTES),
-    )(*in_hbm(args))
-    gates_, ups, downs = gate_proj[0], up_proj[0], down_proj[0]
+    )(core, *in_hbm((*args, gate_proj, up_proj)))
+    came = exchanged(sent)
+    rows_ = pl.pallas_call(
+        turn_kernel,
+        out_shape=rows_of,
+        in_specs=[smem] + [far] * 3,
+        out_specs=far,
+        scratch_shapes=turn_scratch,
+        input_output_aliases={1: 0},
+        cost_estimate=pl.CostEstimate(flops=0, bytes_accessed=32 * shard * width, transcendentals=0),
+        compiler_params=pltpu.CompilerParams(vmem_limit_bytes=VMEM_BYTES),
+    )(core, *in_hbm((rows_, gate_proj, up_proj)))
+    gates_, ups, downs = rows_[:shard], rows_[shard:], down_proj[0]
     weights = (
-        jnp.concatenate([w.T for w in (gates_, swapped(gates_), ups, swapped(ups))], 0),
+        jnp.concatenate([gates_, swapped(gates_), ups, swapped(ups)], 0),
         jnp.concatenate([downs, swapped(downs)], 0),
     )
     hidden = weights[0].shape[0]
     packed = (PAIRS, 2, BLOCK, width // 2 + PACK)
 
-    came = exchanged(sent)
     sent, keep = call(
         experts_first_kernel, [(packed, bf16), ((SHARED, hidden), f32)], came, weights=weights
     )

time: 144 us -> 150 us (1.042)
  the two profiles are of different devices: /device:TPU:224 before, /device:TPU:96 now
where the time goes in v3:
time: 150 us
  blocking collectives  71.3 us (48%)
  waiting for transfers between devices  29.3 us (20%)
  Pallas kernels  23.2 us (15%)
  starting transfers between devices  20.4 us (14%)
  other arithmetic  3.35 us (2%)
  local copies, waits for them, and re-layouts  1.63 us (1%)
    all_to_all x3, blocking collectives, exchanged(): lax.all_to_all(block, ('x', 'y'), split_axis=0, concat_axis=0, tiled=True)  71.3 us
    all_to_all x1, waiting for transfers between devices, exchanged(): lax.all_to_all(block, ('x', 'y'), split_axis=0, concat_axis=0, tiled=True)  23.2 us
    pallas_call x5, Pallas kernels, call(): pl.pallas_call(kernel, out_shape=outs, in_specs=[first] * smem + [spec] *...  16.4 us
    all_to_all x1, starting transfers between devices, exchanged(): lax.all_to_all(block, ('x', 'y'), split_axis=0, concat_axis=0, tiled=True)  7.05 us
    ppermute x2, starting transfers between devices, shifted(): return lax.ppermute(block, 'pipe', route_)  6.96 us
    ppermute x3, starting transfers between devices, swapped(): return lax.ppermute(block, 'core', [(0, 1), (1, 0)])  6.42 us
    ppermute x2, waiting for transfers between devices, shifted(): return lax.ppermute(block, 'pipe', route_)  5.34 us
    pallas_call x1, Pallas kernels, per_device(): pl.pallas_call(prepare_kernel, out_shape=[jax.ShapeDtypeStruct((ROWS, wid...  3.9 us
  transfers between devices with their start and end apart: 6, of which 3 were waited for; matrix products, arithmetic and copies ran while one was open for 3% of the time, Pallas kernels for 2%

profile of v3, /device:TPU:96, one launch (start us, length us, event | category | flops | bytes accessed | tf_op | source)
XLA Modules:
  0.0 150.0 jit_solution(4649292060352799417)
XLA Ops:
  0.6 3.9 %shard_map.131 = (bf16[384,3584]{1,0:T(8,128)(2,1)}, f32[3,8,128]{2,1,0:T(8,128)}, bf16[256,3584]{1,0:T(8,128)(2,1)}) custom-call(s32[1,1]{1,0:T(1,128)} %bitcast.1.core_ref, bf16[1,8,3584]{2,1,0:T(8,128)(2,1)} %x_ref.1, bf16[2,1,8,3584]{3,2,1,0:T(8,128)(2,1)} %s_ref.3, bf16[1,8,3584]{2,1,0:T(8,128)(2,1)} %c_ref.1, bf16[1,3584]{1,0:T(2,128)(2,1)} %gain_ref.5, ...), custom_call_target="tpu_custom_call" | custom-call | tf_op jit(solution)/shard_map/pallas_call | solution.py:426
  4.5 7.0 %all-to-all-start = ((bf16[16,24,3584]{2,1,0:T(8,128)(2,1)}), bf16[16,24,3584]{2,1,0:T(8,128)(2,1)S(1)}, u32[]{:S(2)}, u32[]{:S(2)}) async-start(bf16[16,24,3584]{2,1,0:T(8,128)(2,1)} %bitcast.35), calls=%async_computation | async-start | bytes 5505024 | tf_op jit(solution)/shard_map/all_to_all | solution.py:396
  11.6 2.1 %collective-permute-start.2 = (bf16[128,3584]{1,0:T(8,128)(2,1)}, bf16[128,3584]{1,0:T(8,128)(2,1)S(1)}, u32[]{:S(2)}, u32[]{:S(2)}) collective-permute-start(bf16[128,3584]{1,0:T(8,128)(2,1)} %bitcast.36), channel_id=1, source_target_pairs={{0,1},{1,0},{2,3},{3,2},{4,5},{5,4},{6,7},{7,6},{8,9},{9,8},{10,11... | collective-permute-start | bytes 2752520 | tf_op jit(solution)/shard_map/ppermute | solution.py:391
  13.7 0.0 copy-start.10
  13.7 2.9 %shard_map.132 = bf16[256,3584]{1,0:T(8,128)(2,1)} custom-call(s32[1,1]{1,0:T(1,128)} %bitcast.1.core_ref, bf16[256,3584]{1,0:T(8,128)(2,1)} %get-tuple-element.14.before_hbm, bf16[1,3584,128]{2,1,0:T(8,128)(2,1)} %g_hbm.3, bf16[1,3584,128]{2,1,0:T(8,128)(2,1)} %u_hbm.3), custom_call_target="tpu_custom_call", output_to_operand_aliasing={{}: (1, {})} | custom-call | bytes 14680064 | tf_op jit(solution)/shard_map/pallas_call | solution.py:443
  16.6 1.6 %fusion = (bf16[128,3584]{1,0:T(8,128)(2,1)S(1)}, bf16[128,3584]{1,0:T(8,128)(2,1)S(1)}) fusion(bf16[256,3584]{1,0:T(8,128)(2,1)} %shard_map.132), kind=kLoop, calls=%fused_computation.2 | loop fusion | bytes 3670016 | tf_op jit(solution)/shard_map/slice | solution.py:453
  18.2 1.9 %collective-permute-start = (bf16[128,3584]{1,0:T(8,128)(2,1)S(1)}, bf16[128,3584]{1,0:T(8,128)(2,1)S(1)}, u32[]{:S(2)}, u32[]{:S(2)}) collective-permute-start(bf16[128,3584]{1,0:T(8,128)(2,1)S(1)} %get-tuple-element.24), channel_id=1, source_target_pairs={{0,1},{1,0},{2,3},{3,2},{4,5},{5,4},{6,7},{7,6},{8,9},{9,8},{10,11... | collective-permute-start | bytes 2752520 | tf_op jit(solution)/shard_map/ppermute | solution.py:391
  20.1 2.4 %collective-permute-start.1 = (bf16[128,3584]{1,0:T(8,128)(2,1)S(1)}, bf16[128,3584]{1,0:T(8,128)(2,1)S(1)}, u32[]{:S(2)}, u32[]{:S(2)}) collective-permute-start(bf16[128,3584]{1,0:T(8,128)(2,1)S(1)} %get-tuple-element.25), channel_id=1, source_target_pairs={{0,1},{1,0},{2,3},{3,2},{4,5},{5,4},{6,7},{7,6},{8,9},{9,8},{10,11... | collective-permute-start | bytes 2752520 | tf_op jit(solution)/shard_map/ppermute | solution.py:391
  22.5 0.0 collective-permute-done.2
  22.5 0.0 copy-done.10
  22.5 1.4 pad_maximum_fusion.1.down_hbm
  23.9 0.0 collective-permute-done
  23.9 0.7 collective-permute-done.1
  24.6 2.0 %pad_maximum_fusion.gu_hbm = bf16[512,3584]{1,0:T(8,128)(2,1)} fusion(bf16[128,3584]{1,0:T(8,128)(2,1)S(1)} %collective-permute-done.1, bf16[128,3584]{1,0:T(8,128)(2,1)S(1)} %get-tuple-element.25, bf16[128,3584]{1,0:T(8,128)(2,1)S(1)} %collective-permute-done, bf16[128,3584]{1,0:T(8,128)(2,1)S(1)} %get-tuple-element.24), kind=kLoop, calls=%fused_computation | loop fusion | flops 14680064 | bytes 7340032 | tf_op jit(solution)/shard_map/concatenate | solution.py:455
  26.5 23.2 %all-to-all-done = bf16[16,24,3584]{2,1,0:T(8,128)(2,1)S(1)} async-done(((bf16[16,24,3584]{2,1,0:T(8,128)(2,1)}), bf16[16,24,3584]{2,1,0:T(8,128)(2,1)S(1)}, u32[]{:S(2)}, u32[]{:S(2)}) %all-to-all-start) | async-done | bytes 2752544 | tf_op jit(solution)/shard_map/all_to_all | solution.py:396
  49.8 0.0 copy-start
  49.8 0.0 copy-start.1
  49.8 0.0 copy-start.2
  49.8 0.0 copy-start.3
  49.8 0.0 copy-start.4
  49.8 0.0 copy-start.7
  49.8 0.0 copy-start.8
  49.8 0.0 copy-start.9
  49.8 7.2 %shard_map.133 = (bf16[8,2,24,1920]{3,2,1,0:T(8,128)(2,1)S(1)}, f32[192,512]{1,0:T(8,128)S(1)}) custom-call(bf16[384,3584]{1,0:T(8,128)(2,1)S(1)} %bitcast.16, bf16[512,3584]{1,0:T(8,128)(2,1)} %pad_maximum_fusion.gu_hbm, bf16[256,3584]{1,0:T(8,128)(2,1)} %pad_maximum_fusion.1.down_hbm), custom_call_target="tpu_custom_call" | custom-call | tf_op jit(solution)/shard_map/pallas_call | solution.py:380
  57.0 0.0 copy-start.5
  57.0 0.0 copy-start.6
  57.0 29.9 %all_to_all.44 = bf16[16,24,1920]{2,1,0:T(8,128)(2,1)S(1)} all-to-all(bf16[16,24,1920]{2,1,0:T(8,128)(2,1)S(1)} %bitcast.21), channel_id=1, replica_groups=mesh['pipe'=16,'x'=4,'y'=4,'core'=2] {'x','y'}, dimensions={0} | all-to-all | bytes 2949120 | tf_op jit(solution)/shard_map/all_to_all | solution.py:396
  86.9 0.0 copy-done
  86.9 0.0 copy-done.1
  86.9 0.0 copy-done.2
  86.9 0.0 copy-done.3
  86.9 0.0 copy-done.4
  87.0 0.0 copy-done.7
  87.0 0.0 copy-done.8
  87.0 0.0 copy-done.9
  87.0 1.0 shard_map.134
  88.0 5.0 %collective-permute-start.3 = (bf16[8,3584]{1,0:T(8,128)(2,1)S(1)}, bf16[8,3584]{1,0:T(8,128)(2,1)S(1)}, u32[]{:S(2)}, u32[]{:S(2)}) collective-permute-start(bf16[8,3584]{1,0:T(8,128)(2,1)S(1)} %get-tuple-element.17.y0_ref), channel_id=1, source_target_pairs={{0,32},{32,64},{64,96},{96,128},{128,160},{160,192},{192,224},{224... | collective-permute-start | bytes 172040 | tf_op jit(solution)/shard_map/ppermute | solution.py:402
  93.0 1.9 %collective-permute-start.4 = (bf16[8,3584]{1,0:T(8,128)(2,1)S(1)}, bf16[8,3584]{1,0:T(8,128)(2,1)S(1)}, u32[]{:S(2)}, u32[]{:S(2)}) collective-permute-start(bf16[8,3584]{1,0:T(8,128)(2,1)S(1)} %get-tuple-element.18.b0_ref), channel_id=1, source_target_pairs={{32,0},{64,32},{96,64},{128,96},{160,128},{192,160},{224,192},{256... | collective-permute-start | bytes 172040 | tf_op jit(solution)/shard_map/ppermute | solution.py:402
  95.0 0.0 collective-permute-done.3.y_ref
  95.0 5.3 %collective-permute-done.4.b_ref = bf16[8,3584]{1,0:T(8,128)(2,1)S(1)} collective-permute-done((bf16[8,3584]{1,0:T(8,128)(2,1)S(1)}, bf16[8,3584]{1,0:T(8,128)(2,1)S(1)}, u32[]{:S(2)}, u32[]{:S(2)}) %collective-permute-start.4) | collective-permute-done | bytes 57376 | tf_op jit(solution)/shard_map/ppermute | solution.py:402
  100.3 0.0 copy-done.5
  100.3 0.0 copy-done.6
  100.3 0.7 shard_map.135
  101.1 20.8 %all_to_all.45 = bf16[16,24,1792]{2,1,0:T(8,128)(2,1)S(1)} all-to-all(bf16[16,24,1792]{2,1,0:T(8,128)(2,1)S(1)} %bitcast.22), channel_id=1, replica_groups=mesh['pipe'=16,'x'=4,'y'=4,'core'=2] {'x','y'}, dimensions={0} | all-to-all | bytes 2752512 | tf_op jit(solution)/shard_map/all_to_all | solution.py:396
  121.9 5.9 %shard_map.136 = bf16[8,2,24,1920]{3,2,1,0:T(8,128)(2,1)S(1)} custom-call(bf16[384,1792]{1,0:T(8,128)(2,1)S(1)} %bitcast.20, f32[192,512]{1,0:T(8,128)S(1)} %get-tuple-element.20.keep_ref, bf16[512,3584]{1,0:T(8,128)(2,1)} %pad_maximum_fusion.gu_hbm, bf16[256,3584]{1,0:T(8,128)(2,1)} %pad_maximum_fusion.1.down_hbm), custom_call_target="tpu_custom_call" | custom-call | tf_op jit(solution)/shard_map/pallas_call | solution.py:380
  127.7 20.6 %all_to_all.46 = bf16[16,24,1920]{2,1,0:T(8,128)(2,1)S(1)} all-to-all(bf16[16,24,1920]{2,1,0:T(8,128)(2,1)S(1)} %bitcast.19), channel_id=1, replica_groups=mesh['pipe'=16,'x'=4,'y'=4,'core'=2] {'x','y'}, dimensions={0} | all-to-all | bytes 2949120 | tf_op jit(solution)/shard_map/all_to_all | solution.py:396
  148.3 1.6 %shard_map.137 = (bf16[2,1,8,3584]{3,2,1,0:T(8,128)(2,1)}, bf16[2,1,8,3584]{3,2,1,0:T(8,128)(2,1)}) custom-call(bf16[384,1920]{1,0:T(8,128)(2,1)S(1)} %bitcast.17, bf16[8,3584]{1,0:T(8,128)(2,1)S(1)} %get-tuple-element.21.x_ref, bf16[2,1,8,3584]{3,2,1,0:T(8,128)(2,1)S(1)} %copy-done, bf16[8,3584]{1,0:T(8,128)(2,1)S(1)} %get-tuple-element.22.c_ref, ...), custom_call_target="tpu_custom_call" | custom-call | tf_op jit(solution)/shard_map/pallas_call | solution.py:380
Async XLA Ops:
  4.5 45.2 %all-to-all-start = ((bf16[16,24,3584]{2,1,0:T(8,128)(2,1)}), bf16[16,24,3584]{2,1,0:T(8,128)(2,1)S(1)}, u32[]{:S(2)}, u32[]{:S(2)}) async-start(bf16[16,24,3584]{2,1,0:T(8,128)(2,1)} %bitcast.35), calls=%async_computation | async-start | bytes 5505024 | tf_op jit(solution)/shard_map/all_to_all | solution.py:396
  11.6 10.9 %collective-permute-start.2 = (bf16[128,3584]{1,0:T(8,128)(2,1)}, bf16[128,3584]{1,0:T(8,128)(2,1)S(1)}, u32[]{:S(2)}, u32[]{:S(2)}) collective-permute-start(bf16[128,3584]{1,0:T(8,128)(2,1)} %bitcast.36), channel_id=1, source_target_pairs={{0,1},{1,0},{2,3},{3,2},{4,5},{5,4},{6,7},{7,6},{8,9},{9,8},{10,11... | collective-permute-start | bytes 2752520 | tf_op jit(solution)/shard_map/ppermute | solution.py:391
  13.7 8.8 %copy-start.10 = (bf16[1,128,3584]{2,1,0:T(8,128)(2,1)S(1)}, bf16[1,128,3584]{2,1,0:T(8,128)(2,1)}, u32[]{:S(2)}) copy-start(bf16[1,128,3584]{2,1,0:T(8,128)(2,1)} %param.23) | copy-start | bytes 2752516
  18.2 5.8 %collective-permute-start = (bf16[128,3584]{1,0:T(8,128)(2,1)S(1)}, bf16[128,3584]{1,0:T(8,128)(2,1)S(1)}, u32[]{:S(2)}, u32[]{:S(2)}) collective-permute-start(bf16[128,3584]{1,0:T(8,128)(2,1)S(1)} %get-tuple-element.24), channel_id=1, source_target_pairs={{0,1},{1,0},{2,3},{3,2},{4,5},{5,4},{6,7},{7,6},{8,9},{9,8},{10,11... | collective-permute-start | bytes 2752520 | tf_op jit(solution)/shard_map/ppermute | solution.py:391
  20.1 4.5 %collective-permute-start.1 = (bf16[128,3584]{1,0:T(8,128)(2,1)S(1)}, bf16[128,3584]{1,0:T(8,128)(2,1)S(1)}, u32[]{:S(2)}, u32[]{:S(2)}) collective-permute-start(bf16[128,3584]{1,0:T(8,128)(2,1)S(1)} %get-tuple-element.25), channel_id=1, source_target_pairs={{0,1},{1,0},{2,3},{3,2},{4,5},{5,4},{6,7},{7,6},{8,9},{9,8},{10,11... | collective-permute-start | bytes 2752520 | tf_op jit(solution)/shard_map/ppermute | solution.py:391
  49.8 37.1 %copy-start = (bf16[2,1,8,3584]{3,2,1,0:T(8,128)(2,1)S(1)}, bf16[2,1,8,3584]{3,2,1,0:T(8,128)(2,1)}, u32[]{:S(2)}) copy-start(bf16[2,1,8,3584]{3,2,1,0:T(8,128)(2,1)} %s_ref.3) | copy-start | bytes 344068
  49.8 37.1 %copy-start.1 = (bf16[1,3584,4]{1,2,0:T(4,128)(2,1)S(1)}, bf16[1,3584,4]{1,2,0:T(4,128)(2,1)}, u32[]{:S(2)}) copy-start(bf16[1,3584,4]{1,2,0:T(4,128)(2,1)} %param.20) | copy-start | bytes 86020
  49.8 37.1 %copy-start.2 = (bf16[1,8,3584]{2,1,0:T(8,128)(2,1)S(1)}, bf16[1,8,3584]{2,1,0:T(8,128)(2,1)}, u32[]{:S(2)}) copy-start(bf16[1,8,3584]{2,1,0:T(8,128)(2,1)} %x_ref.1) | copy-start | bytes 172036
  49.8 37.2 %copy-start.3 = (bf16[1,8,3584]{2,1,0:T(8,128)(2,1)S(1)}, bf16[1,8,3584]{2,1,0:T(8,128)(2,1)}, u32[]{:S(2)}) copy-start(bf16[1,8,3584]{2,1,0:T(8,128)(2,1)} %c_ref.1) | copy-start | bytes 172036
  49.8 37.2 %copy-start.4 = (bf16[1,3584]{1,0:T(2,128)(2,1)S(1)}, bf16[1,3584]{1,0:T(2,128)(2,1)}, u32[]{:S(2)}) copy-start(bf16[1,3584]{1,0:T(2,128)(2,1)} %gain_ref.5) | copy-start | bytes 21508
  49.8 37.2 %copy-start.7 = (f32[3,8,128]{2,1,0:T(8,128)S(1)}, f32[3,8,128]{2,1,0:T(8,128)}, u32[]{:S(2)}) copy-start(f32[3,8,128]{2,1,0:T(8,128)} %get-tuple-element.16.stat_ref) | copy-start | bytes 36868
  49.8 37.2 %copy-start.8 = (s32[2,1,8,2]{2,3,1,0:T(2,128)S(1)}, s32[2,1,8,2]{2,3,1,0:T(2,128)}, u32[]{:S(2)}) copy-start(s32[2,1,8,2]{2,3,1,0:T(2,128)} %param.17) | copy-start | bytes 388
  49.8 37.2 %copy-start.9 = (s32[2,1,8,2]{2,3,1,0:T(2,128)S(1)}, s32[2,1,8,2]{2,3,1,0:T(2,128)}, u32[]{:S(2)}) copy-start(s32[2,1,8,2]{2,3,1,0:T(2,128)} %param.18) | copy-start | bytes 388
  57.0 43.3 %copy-start.5 = (bf16[1,8,3584]{2,1,0:T(8,128)(2,1)S(1)}, bf16[1,8,3584]{2,1,0:T(8,128)(2,1)}, u32[]{:S(2)}) copy-start(bf16[1,8,3584]{2,1,0:T(8,128)(2,1)} %fnew_ref.1) | copy-start | bytes 172036
  57.0 43.3 %copy-start.6 = (bf16[1,8,3584]{2,1,0:T(8,128)(2,1)S(1)}, bf16[1,8,3584]{2,1,0:T(8,128)(2,1)}, u32[]{:S(2)}) copy-start(bf16[1,8,3584]{2,1,0:T(8,128)(2,1)} %gnew_ref.1) | copy-start | bytes 172036
  88.0 7.0 %collective-permute-start.3 = (bf16[8,3584]{1,0:T(8,128)(2,1)S(1)}, bf16[8,3584]{1,0:T(8,128)(2,1)S(1)}, u32[]{:S(2)}, u32[]{:S(2)}) collective-permute-start(bf16[8,3584]{1,0:T(8,128)(2,1)S(1)} %get-tuple-element.17.y0_ref), channel_id=1, source_target_pairs={{0,32},{32,64},{64,96},{96,128},{128,160},{160,192},{192,224},{224... | collective-permute-start | bytes 172040 | tf_op jit(solution)/shard_map/ppermute | solution.py:402
  93.0 7.3 %collective-permute-start.4 = (bf16[8,3584]{1,0:T(8,128)(2,1)S(1)}, bf16[8,3584]{1,0:T(8,128)(2,1)S(1)}, u32[]{:S(2)}, u32[]{:S(2)}) collective-permute-start(bf16[8,3584]{1,0:T(8,128)(2,1)S(1)} %get-tuple-element.18.b0_ref), channel_id=1, source_target_pairs={{32,0},{64,32},{96,64},{128,96},{160,128},{192,160},{224,192},{256... | collective-permute-start | bytes 172040 | tf_op jit(solution)/shard_map/ppermute | solution.py:402

commit v4 on v2

--- a/solution.py
+++ b/solution.py
@@ -119,12 +119,15 @@
         rows.append(normed)
     stacked = jnp.concatenate([rows[0], rows[1], c_ref[0].astype(f32), rows[2]], 0).astype(bf16)
     step = ROWS // EXPERTS
+    part = step // 2
     sends = []
     for e in range(EXPERTS):
-        at = pl.ds(e * step, step)
-        out_ref[at] = dot(table[e * step : (e + 1) * step].astype(bf16), stacked).astype(bf16)
-        sends.append(pltpu.make_async_copy(out_ref.at[at], out_hbm.at[at], out_sem.at[e]))
-        sends[-1].start()
+        at = pl.ds(e * part, part)
+        out_ref[at] = dot(table[e * step : e * step + part].astype(bf16), stacked).astype(bf16)
+        for n in range(2):
+            place = out_hbm.at[pl.ds(e * step + n * part, part)]
+            sends.append(pltpu.make_async_copy(out_ref.at[at], place, out_sem.at[2 * e + n]))
+            sends[-1].start()
     for send in sends:
         send.wait()
 
@@ -388,9 +391,9 @@
         out_specs=[pl.BlockSpec(memory_space=pltpu.HBM), pl.BlockSpec(memory_space=pltpu.VMEM)],
         scratch_shapes=[pltpu.VMEM(a.shape, a.dtype) for a in args]
         + [
-            pltpu.VMEM((ROWS, width), bf16),
+            pltpu.VMEM((ROWS // 2, width), bf16),
             pltpu.SemaphoreType.DMA((len(args),)),
-            pltpu.SemaphoreType.DMA((EXPERTS,)),
+            pltpu.SemaphoreType.DMA((2 * EXPERTS,)),
         ],
         compiler_params=pltpu.CompilerParams(vmem_limit_bytes=PREPARE_BYTES),
     )(*in_hbm(args))

time: 144 us -> 144 us (level)
  no operation moved by 1% of the time
where the time goes in v4:
time: 144 us; the launch traced here: 143 us
  blocking collectives  64.5 us (45%)
  waiting for transfers between devices  27.1 us (19%)
  starting transfers between devices  20.4 us (14%)
  Pallas kernels  20.2 us (14%)
  other arithmetic  5.83 us (4%)
  local copies, waits for them, and re-layouts  4.61 us (3%)
    all_to_all x3, blocking collectives, exchanged(): lax.all_to_all(block, ('x', 'y'), split_axis=0, concat_axis=0, tiled=True)  64.5 us
    all_to_all x1, waiting for transfers between devices, exchanged(): lax.all_to_all(block, ('x', 'y'), split_axis=0, concat_axis=0, tiled=True)  21.7 us
    pallas_call x5, Pallas kernels, call(): pl.pallas_call(kernel, out_shape=outs, in_specs=[first] * smem + [spec] *...  16.4 us
    all_to_all x1, starting transfers between devices, exchanged(): lax.all_to_all(block, ('x', 'y'), split_axis=0, concat_axis=0, tiled=True)  7.05 us
    ppermute x2, starting transfers between devices, shifted(): return lax.ppermute(block, 'pipe', route_)  6.95 us
    ppermute x3, starting transfers between devices, swapped(): return lax.ppermute(block, 'core', [(0, 1), (1, 0)])  6.36 us
    ppermute x2, waiting for transfers between devices, shifted(): return lax.ppermute(block, 'pipe', route_)  5.34 us
    unnamed x26, local copies, waits for them, and re-layouts  4.61 us
  transfers between devices with their start and end apart: 6, of which 2 were waited for; matrix products, arithmetic and copies ran while one was open for 7% of the time, Pallas kernels for 0%

profile of v4, /device:TPU:224, one launch (start us, length us, event | category | flops | bytes accessed | tf_op | source)
XLA Modules:
  0.0 143.4 jit_solution(5544930658127259619)
XLA Ops:
  0.6 3.7 %shard_map.131 = (bf16[384,3584]{1,0:T(8,128)(2,1)}, f32[3,8,128]{2,1,0:T(8,128)}) custom-call(bf16[1,8,3584]{2,1,0:T(8,128)(2,1)} %x_ref.1, bf16[2,1,8,3584]{3,2,1,0:T(8,128)(2,1)} %s_ref.3, bf16[1,8,3584]{2,1,0:T(8,128)(2,1)} %c_ref.1, bf16[1,3584]{1,0:T(2,128)(2,1)} %gain_ref.5, bf16[4,3584]{1,0:T(4,128)(2,1)} %bitcast.30, s32[2,1,2,8]{3,2,1,0:T(2,128)} %bitcast.34, ...), custom_call_target="tpu_custom_call" | custom-call | tf_op jit(solution)/shard_map/pallas_call | solution.py:387
  4.4 7.0 %all-to-all-start = ((bf16[16,24,3584]{2,1,0:T(8,128)(2,1)}), bf16[16,24,3584]{2,1,0:T(8,128)(2,1)S(1)}, u32[]{:S(2)}, u32[]{:S(2)}) async-start(bf16[16,24,3584]{2,1,0:T(8,128)(2,1)} %bitcast.46), calls=%async_computation | async-start | bytes 5505024 | tf_op jit(solution)/shard_map/all_to_all | solution.py:367
  11.4 1.9 %collective-permute-start.2 = (bf16[128,3584]{1,0:T(8,128)(2,1)}, bf16[128,3584]{1,0:T(8,128)(2,1)}, u32[]{:S(2)}, u32[]{:S(2)}) collective-permute-start(bf16[128,3584]{1,0:T(8,128)(2,1)} %bitcast.47), channel_id=1, source_target_pairs={{0,1},{1,0},{2,3},{3,2},{4,5},{5,4},{6,7},{7,6},{8,9},{9,8},{10,11... | collective-permute-start | bytes 2752520 | tf_op jit(solution)/shard_map/ppermute | solution.py:362
  13.4 2.3 %copy.15 = bf16[1,3584,128]{1,2,0:T(8,128)(2,1)} copy(bf16[1,3584,128]{2,1,0:T(8,128)(2,1)} %param.22) | data formatting | bytes 1835008 | tf_op args[10]
  15.7 2.4 %collective-permute-start.1 = (bf16[3584,128]{0,1:T(8,128)(2,1)}, bf16[3584,128]{0,1:T(8,128)(2,1)}, u32[]{:S(2)}, u32[]{:S(2)}) collective-permute-start(bf16[3584,128]{0,1:T(8,128)(2,1)} %bitcast.42), channel_id=1, source_target_pairs={{0,1},{1,0},{2,3},{3,2},{4,5},{5,4},{6,7},{7,6},{8,9},{9,8},{10,11... | collective-permute-start | bytes 2752520 | tf_op jit(solution)/shard_map/ppermute | solution.py:362
  18.1 2.3 %copy.14 = bf16[1,3584,128]{1,2,0:T(8,128)(2,1)} copy(bf16[1,3584,128]{2,1,0:T(8,128)(2,1)} %param.21) | data formatting | bytes 1835008 | tf_op args[9]
  20.3 0.0 copy-start.10
  20.3 0.0 copy-start.11
  20.3 2.0 %collective-permute-start = (bf16[3584,128]{0,1:T(8,128)(2,1)}, bf16[3584,128]{0,1:T(8,128)(2,1)S(1)}, u32[]{:S(2)}, u32[]{:S(2)}) collective-permute-start(bf16[3584,128]{0,1:T(8,128)(2,1)} %bitcast.44), channel_id=1, source_target_pairs={{0,1},{1,0},{2,3},{3,2},{4,5},{5,4},{6,7},{7,6},{8,9},{9,8},{10,11... | collective-permute-start | bytes 2752520 | tf_op jit(solution)/shard_map/ppermute | solution.py:362
  22.4 0.0 collective-permute-done.2
  22.4 2.8 %pad_maximum_fusion.1.down_hbm = bf16[256,3584]{1,0:T(8,128)(2,1)} fusion(bf16[128,3584]{1,0:T(8,128)(2,1)} %collective-permute-done.2, bf16[128,3584]{1,0:T(8,128)(2,1)} %bitcast.48), kind=kLoop, calls=%fused_computation.1 | loop fusion | flops 3670016 | bytes 3670016 | tf_op jit(solution)/shard_map/concatenate | solution.py:403
  25.2 0.0 collective-permute-done.1
  25.2 0.0 collective-permute-done
  25.2 0.0 copy-done.10
  25.2 0.0 copy-done.11
  25.2 3.0 %pad_maximum_fusion.gu_hbm = bf16[512,3584]{1,0:T(8,128)(2,1)} fusion(bf16[128,3584]{1,0:T(8,128)(2,1)} %bitcast.12, bf16[128,3584]{1,0:T(8,128)(2,1)S(1)} %bitcast.43, bf16[128,3584]{1,0:T(8,128)(2,1)S(1)} %bitcast.49, bf16[128,3584]{1,0:T(8,128)(2,1)S(1)} %bitcast.45), kind=kLoop, calls=%fused_computation | loop fusion | flops 14680064 | bytes 7340032 | tf_op jit(solution)/shard_map/concatenate | solution.py:402
  28.2 21.7 %all-to-all-done = bf16[16,24,3584]{2,1,0:T(8,128)(2,1)S(1)} async-done(((bf16[16,24,3584]{2,1,0:T(8,128)(2,1)}), bf16[16,24,3584]{2,1,0:T(8,128)(2,1)S(1)}, u32[]{:S(2)}, u32[]{:S(2)}) %all-to-all-start) | async-done | bytes 2752544 | tf_op jit(solution)/shard_map/all_to_all | solution.py:367
  50.0 0.0 copy-start
  50.0 0.0 copy-start.1
  50.0 0.0 copy-start.2
  50.0 0.0 copy-start.4
  50.0 0.0 copy-start.7
  50.0 0.0 copy-start.8
  50.0 0.0 copy-start.9
  50.0 7.2 %shard_map.132 = (bf16[8,2,24,1920]{3,2,1,0:T(8,128)(2,1)S(1)}, f32[192,512]{1,0:T(8,128)S(1)}) custom-call(bf16[384,3584]{1,0:T(8,128)(2,1)S(1)} %bitcast.23, bf16[512,3584]{1,0:T(8,128)(2,1)} %pad_maximum_fusion.gu_hbm, bf16[256,3584]{1,0:T(8,128)(2,1)} %pad_maximum_fusion.1.down_hbm), custom_call_target="tpu_custom_call" | custom-call | tf_op jit(solution)/shard_map/pallas_call | solution.py:351
  57.2 0.0 copy-start.5
  57.2 0.0 copy-start.6
  57.2 24.9 %all_to_all.44 = bf16[16,24,1920]{2,1,0:T(8,128)(2,1)S(1)} all-to-all(bf16[16,24,1920]{2,1,0:T(8,128)(2,1)S(1)} %bitcast.28), channel_id=1, replica_groups=mesh['pipe'=16,'x'=4,'y'=4,'core'=2] {'x','y'}, dimensions={0} | all-to-all | bytes 2949120 | tf_op jit(solution)/shard_map/all_to_all | solution.py:367
  82.2 0.0 copy-done
  82.2 0.0 copy-done.1
  82.2 0.0 copy-done.2
  82.2 0.0 copy-done.3
  82.2 0.0 copy-done.4
  82.2 0.0 copy-done.7
  82.2 0.0 copy-done.8
  82.2 0.0 copy-done.9
  82.2 1.0 shard_map.133
  83.2 5.0 %collective-permute-start.3 = (bf16[8,3584]{1,0:T(8,128)(2,1)S(1)}, bf16[8,3584]{1,0:T(8,128)(2,1)S(1)}, u32[]{:S(2)}, u32[]{:S(2)}) collective-permute-start(bf16[8,3584]{1,0:T(8,128)(2,1)S(1)} %get-tuple-element.15.y0_ref), channel_id=1, source_target_pairs={{0,32},{32,64},{64,96},{96,128},{128,160},{160,192},{192,224},{224... | collective-permute-start | bytes 172040 | tf_op jit(solution)/shard_map/ppermute | solution.py:373
  88.3 1.9 %collective-permute-start.4 = (bf16[8,3584]{1,0:T(8,128)(2,1)S(1)}, bf16[8,3584]{1,0:T(8,128)(2,1)S(1)}, u32[]{:S(2)}, u32[]{:S(2)}) collective-permute-start(bf16[8,3584]{1,0:T(8,128)(2,1)S(1)} %get-tuple-element.16.b0_ref), channel_id=1, source_target_pairs={{32,0},{64,32},{96,64},{128,96},{160,128},{192,160},{224,192},{256... | collective-permute-start | bytes 172040 | tf_op jit(solution)/shard_map/ppermute | solution.py:373
  90.2 0.0 collective-permute-done.3.y_ref
  90.2 5.3 %collective-permute-done.4.b_ref = bf16[8,3584]{1,0:T(8,128)(2,1)S(1)} collective-permute-done((bf16[8,3584]{1,0:T(8,128)(2,1)S(1)}, bf16[8,3584]{1,0:T(8,128)(2,1)S(1)}, u32[]{:S(2)}, u32[]{:S(2)}) %collective-permute-start.4) | collective-permute-done | bytes 57376 | tf_op jit(solution)/shard_map/ppermute | solution.py:373
  95.6 0.0 copy-done.5
  95.6 0.0 copy-done.6
  95.6 0.7 shard_map.134
  96.3 19.9 %all_to_all.45 = bf16[16,24,1792]{2,1,0:T(8,128)(2,1)S(1)} all-to-all(bf16[16,24,1792]{2,1,0:T(8,128)(2,1)S(1)} %bitcast.29), channel_id=1, replica_groups=mesh['pipe'=16,'x'=4,'y'=4,'core'=2] {'x','y'}, dimensions={0} | all-to-all | bytes 2752512 | tf_op jit(solution)/shard_map/all_to_all | solution.py:367
  116.3 5.9 %shard_map.135 = bf16[8,2,24,1920]{3,2,1,0:T(8,128)(2,1)S(1)} custom-call(bf16[384,1792]{1,0:T(8,128)(2,1)S(1)} %bitcast.27, f32[192,512]{1,0:T(8,128)S(1)} %get-tuple-element.18.keep_ref, bf16[512,3584]{1,0:T(8,128)(2,1)} %pad_maximum_fusion.gu_hbm, bf16[256,3584]{1,0:T(8,128)(2,1)} %pad_maximum_fusion.1.down_hbm), custom_call_target="tpu_custom_call" | custom-call | tf_op jit(solution)/shard_map/pallas_call | solution.py:351
  122.1 19.6 %all_to_all.46 = bf16[16,24,1920]{2,1,0:T(8,128)(2,1)S(1)} all-to-all(bf16[16,24,1920]{2,1,0:T(8,128)(2,1)S(1)} %bitcast.26), channel_id=1, replica_groups=mesh['pipe'=16,'x'=4,'y'=4,'core'=2] {'x','y'}, dimensions={0} | all-to-all | bytes 2949120 | tf_op jit(solution)/shard_map/all_to_all | solution.py:367
  141.7 1.6 %shard_map.136 = (bf16[2,1,8,3584]{3,2,1,0:T(8,128)(2,1)}, bf16[2,1,8,3584]{3,2,1,0:T(8,128)(2,1)}) custom-call(bf16[384,1920]{1,0:T(8,128)(2,1)S(1)} %bitcast.24, bf16[8,3584]{1,0:T(8,128)(2,1)S(1)} %get-tuple-element.19.x_ref, bf16[2,1,8,3584]{3,2,1,0:T(8,128)(2,1)S(1)} %copy-done, bf16[8,3584]{1,0:T(8,128)(2,1)S(1)} %get-tuple-element.20.c_ref, ...), custom_call_target="tpu_custom_call" | custom-call | tf_op jit(solution)/shard_map/pallas_call | solution.py:351
  (1 shorter events, 0.0 us)
Async XLA Ops:
  4.4 45.6 %all-to-all-start = ((bf16[16,24,3584]{2,1,0:T(8,128)(2,1)}), bf16[16,24,3584]{2,1,0:T(8,128)(2,1)S(1)}, u32[]{:S(2)}, u32[]{:S(2)}) async-start(bf16[16,24,3584]{2,1,0:T(8,128)(2,1)} %bitcast.46), calls=%async_computation | async-start | bytes 5505024 | tf_op jit(solution)/shard_map/all_to_all | solution.py:367
  11.4 10.9 %collective-permute-start.2 = (bf16[128,3584]{1,0:T(8,128)(2,1)}, bf16[128,3584]{1,0:T(8,128)(2,1)}, u32[]{:S(2)}, u32[]{:S(2)}) collective-permute-start(bf16[128,3584]{1,0:T(8,128)(2,1)} %bitcast.47), channel_id=1, source_target_pairs={{0,1},{1,0},{2,3},{3,2},{4,5},{5,4},{6,7},{7,6},{8,9},{9,8},{10,11... | collective-permute-start | bytes 2752520 | tf_op jit(solution)/shard_map/ppermute | solution.py:362
  15.7 9.6 %collective-permute-start.1 = (bf16[3584,128]{0,1:T(8,128)(2,1)}, bf16[3584,128]{0,1:T(8,128)(2,1)}, u32[]{:S(2)}, u32[]{:S(2)}) collective-permute-start(bf16[3584,128]{0,1:T(8,128)(2,1)} %bitcast.42), channel_id=1, source_target_pairs={{0,1},{1,0},{2,3},{3,2},{4,5},{5,4},{6,7},{7,6},{8,9},{9,8},{10,11... | collective-permute-start | bytes 2752520 | tf_op jit(solution)/shard_map/ppermute | solution.py:362
  20.3 4.9 %copy-start.10 = (bf16[1,3584,128]{1,2,0:T(8,128)(2,1)S(1)}, bf16[1,3584,128]{1,2,0:T(8,128)(2,1)}, u32[]{:S(2)}) copy-start(bf16[1,3584,128]{1,2,0:T(8,128)(2,1)} %copy.15) | copy-start | bytes 2752516
  20.3 4.9 %copy-start.11 = (bf16[1,3584,128]{1,2,0:T(8,128)(2,1)S(1)}, bf16[1,3584,128]{1,2,0:T(8,128)(2,1)}, u32[]{:S(2)}) copy-start(bf16[1,3584,128]{1,2,0:T(8,128)(2,1)} %copy.14) | copy-start | bytes 2752516
  20.3 4.9 %collective-permute-start = (bf16[3584,128]{0,1:T(8,128)(2,1)}, bf16[3584,128]{0,1:T(8,128)(2,1)S(1)}, u32[]{:S(2)}, u32[]{:S(2)}) collective-permute-start(bf16[3584,128]{0,1:T(8,128)(2,1)} %bitcast.44), channel_id=1, source_target_pairs={{0,1},{1,0},{2,3},{3,2},{4,5},{5,4},{6,7},{7,6},{8,9},{9,8},{10,11... | collective-permute-start | bytes 2752520 | tf_op jit(solution)/shard_map/ppermute | solution.py:362
  50.0 32.2 %copy-start = (bf16[2,1,8,3584]{3,2,1,0:T(8,128)(2,1)S(1)}, bf16[2,1,8,3584]{3,2,1,0:T(8,128)(2,1)}, u32[]{:S(2)}) copy-start(bf16[2,1,8,3584]{3,2,1,0:T(8,128)(2,1)} %s_ref.3) | copy-start | bytes 344068
  50.0 32.2 %copy-start.1 = (bf16[1,3584,4]{1,2,0:T(4,128)(2,1)S(1)}, bf16[1,3584,4]{1,2,0:T(4,128)(2,1)}, u32[]{:S(2)}) copy-start(bf16[1,3584,4]{1,2,0:T(4,128)(2,1)} %param.20) | copy-start | bytes 86020
  50.0 32.2 %copy-start.2 = (bf16[1,8,3584]{2,1,0:T(8,128)(2,1)S(1)}, bf16[1,8,3584]{2,1,0:T(8,128)(2,1)}, u32[]{:S(2)}) copy-start(bf16[1,8,3584]{2,1,0:T(8,128)(2,1)} %x_ref.1) | copy-start | bytes 172036
  50.0 32.2 %copy-start.3 = (bf16[1,8,3584]{2,1,0:T(8,128)(2,1)S(1)}, bf16[1,8,3584]{2,1,0:T(8,128)(2,1)}, u32[]{:S(2)}) copy-start(bf16[1,8,3584]{2,1,0:T(8,128)(2,1)} %c_ref.1) | copy-start | bytes 172036
  50.0 32.2 %copy-start.4 = (bf16[1,3584]{1,0:T(2,128)(2,1)S(1)}, bf16[1,3584]{1,0:T(2,128)(2,1)}, u32[]{:S(2)}) copy-start(bf16[1,3584]{1,0:T(2,128)(2,1)} %gain_ref.5) | copy-start | bytes 21508
  50.0 32.2 %copy-start.7 = (f32[3,8,128]{2,1,0:T(8,128)S(1)}, f32[3,8,128]{2,1,0:T(8,128)}, u32[]{:S(2)}) copy-start(f32[3,8,128]{2,1,0:T(8,128)} %get-tuple-element.14.stat_ref) | copy-start | bytes 36868
  50.0 32.2 %copy-start.8 = (s32[2,1,8,2]{2,3,1,0:T(2,128)S(1)}, s32[2,1,8,2]{2,3,1,0:T(2,128)}, u32[]{:S(2)}) copy-start(s32[2,1,8,2]{2,3,1,0:T(2,128)} %param.17) | copy-start | bytes 388
  50.0 32.2 %copy-start.9 = (s32[2,1,8,2]{2,3,1,0:T(2,128)S(1)}, s32[2,1,8,2]{2,3,1,0:T(2,128)}, u32[]{:S(2)}) copy-start(s32[2,1,8,2]{2,3,1,0:T(2,128)} %param.18) | copy-start | bytes 388
  57.2 38.3 %copy-start.5 = (bf16[1,8,3584]{2,1,0:T(8,128)(2,1)S(1)}, bf16[1,8,3584]{2,1,0:T(8,128)(2,1)}, u32[]{:S(2)}) copy-start(bf16[1,8,3584]{2,1,0:T(8,128)(2,1)} %fnew_ref.1) | copy-start | bytes 172036
  57.2 38.3 %copy-start.6 = (bf16[1,8,3584]{2,1,0:T(8,128)(2,1)S(1)}, bf16[1,8,3584]{2,1,0:T(8,128)(2,1)}, u32[]{:S(2)}) copy-start(bf16[1,8,3584]{2,1,0:T(8,128)(2,1)} %gnew_ref.1) | copy-start | bytes 172036
  83.2 7.0 %collective-permute-start.3 = (bf16[8,3584]{1,0:T(8,128)(2,1)S(1)}, bf16[8,3584]{1,0:T(8,128)(2,1)S(1)}, u32[]{:S(2)}, u32[]{:S(2)}) collective-permute-start(bf16[8,3584]{1,0:T(8,128)(2,1)S(1)} %get-tuple-element.15.y0_ref), channel_id=1, source_target_pairs={{0,32},{32,64},{64,96},{96,128},{128,160},{160,192},{192,224},{224... | collective-permute-start | bytes 172040 | tf_op jit(solution)/shard_map/ppermute | solution.py:373
  88.3 7.3 %collective-permute-start.4 = (bf16[8,3584]{1,0:T(8,128)(2,1)S(1)}, bf16[8,3584]{1,0:T(8,128)(2,1)S(1)}, u32[]{:S(2)}, u32[]{:S(2)}) collective-permute-start(bf16[8,3584]{1,0:T(8,128)(2,1)S(1)} %get-tuple-element.16.b0_ref), channel_id=1, source_target_pairs={{32,0},{64,32},{96,64},{128,96},{160,128},{192,160},{224,192},{256... | collective-permute-start | bytes 172040 | tf_op jit(solution)/shard_map/ppermute | solution.py:373

commit v5 on v4

--- a/solution.py
+++ b/solution.py
@@ -217,7 +217,7 @@
             pltpu.make_async_copy(gu_hbm.at[:, a], gu_ref.at[:, a], sems.at[n]) for n, a in enumerate(at)
         ]
         self.copies.append(pltpu.make_async_copy(down_hbm, down_ref, sems.at[CHUNKS]))
-        for copy in self.copies:
+        for copy in self.copies[-1:] + self.copies[:-1]:
             copy.start()
 
     def wait(self, n):
@@ -226,20 +226,23 @@
 
 def experts_first_kernel(in_ref, gu_hbm, down_hbm, out_ref, keep_ref, gu_ref, down_ref, sems):
     weights = Weights(gu_hbm, down_hbm, gu_ref, down_ref, sems)
+    weights.wait(CHUNKS)
+    grad_act = squeezed(roll_up(dot_nt(in_ref[...], down_ref[...]), CAP))
     pre = 0.0
     for n in range(CHUNKS):
         weights.wait(n)
         at = slice(n * weights.chunk, (n + 1) * weights.chunk)
         pre = pre + dot_nt(in_ref[:, at], gu_ref[:, at])
     keep_ref[...] = squeezed(roll_up(pre, 2 * CAP))
-    weights.wait(CHUNKS)
-    grad_act = squeezed(roll_up(dot_nt(in_ref[...], down_ref[...]), CAP))
     experts(squeezed(pre), grad_act, gu_ref, down_ref, out_ref)
 
 
 def experts_second_kernel(in_ref, keep_ref, gu_hbm, down_hbm, out_ref, gu_ref, down_ref, sems):
     weights = Weights(gu_hbm, down_hbm, gu_ref, down_ref, sems)
     width = in_ref.shape[1]
+    weights.wait(CHUNKS)
+    rows = in_ref[...]
+    grad_act = dot_nt(rows, down_ref[:, :width]) + roll_up(dot_nt(rows, down_ref[:, width:]), 2 * CAP)
     sides = [0.0, 0.0]
     for n in range(CHUNKS):
         weights.wait(n)
@@ -247,9 +250,6 @@
         part = dot_nt(in_ref[:, at : at + weights.chunk], gu_ref[:, n * weights.chunk : (n + 1) * weights.chunk])
         sides[h] = sides[h] + part
     pre = squeezed(sides[0] + roll_up(sides[1], 2 * CAP))
-    weights.wait(CHUNKS)
-    rows = in_ref[...]
-    grad_act = dot_nt(rows, down_ref[:, :width]) + roll_up(dot_nt(rows, down_ref[:, width:]), 2 * CAP)
     early, offset = early_half(pre.shape[1])
     forward = jnp.where(early, offset, offset - 2 * CAP) < CAP
     pre = jnp.where(forward, pre, keep_ref[...])

time: 144 us -> 146 us (1.014)
  Pallas kernels: 20.2 us -> 22.3 us
    pallas_call x5, Pallas kernels: 16.4 us -> 18.6 us  [call(): pl.pallas_call(kernel, out_shape=outs, in_specs=[first] * smem + [spec] *...]
where the time goes in v5:
time: 146 us
  blocking collectives  64.5 us (44%)
  waiting for transfers between devices  27.1 us (19%)
  Pallas kernels  22.3 us (15%)
  starting transfers between devices  20.4 us (14%)
  other arithmetic  5.83 us (4%)
  local copies, waits for them, and re-layouts  4.61 us (3%)
    all_to_all x3, blocking collectives, exchanged(): lax.all_to_all(block, ('x', 'y'), split_axis=0, concat_axis=0, tiled=True)  64.5 us
    all_to_all x1, waiting for transfers between devices, exchanged(): lax.all_to_all(block, ('x', 'y'), split_axis=0, concat_axis=0, tiled=True)  21.7 us
    pallas_call x5, Pallas kernels, call(): pl.pallas_call(kernel, out_shape=outs, in_specs=[first] * smem + [spec] *...  18.6 us
    all_to_all x1, starting transfers between devices, exchanged(): lax.all_to_all(block, ('x', 'y'), split_axis=0, concat_axis=0, tiled=True)  7.05 us
    ppermute x2, starting transfers between devices, shifted(): return lax.ppermute(block, 'pipe', route_)  6.96 us
    ppermute x3, starting transfers between devices, swapped(): return lax.ppermute(block, 'core', [(0, 1), (1, 0)])  6.36 us
    ppermute x2, waiting for transfers between devices, shifted(): return lax.ppermute(block, 'pipe', route_)  5.34 us
    unnamed x26, local copies, waits for them, and re-layouts  4.61 us
  transfers between devices with their start and end apart: 6, of which 2 were waited for; matrix products, arithmetic and copies ran while one was open for 7% of the time, Pallas kernels for 0%

profile of v5, /device:TPU:224, one launch (start us, length us, event | category | flops | bytes accessed | tf_op | source)
XLA Modules:
  0.0 145.5 jit_solution(17283441718666273411)
XLA Ops:
  0.6 3.7 %shard_map.131 = (bf16[384,3584]{1,0:T(8,128)(2,1)}, f32[3,8,128]{2,1,0:T(8,128)}) custom-call(bf16[1,8,3584]{2,1,0:T(8,128)(2,1)} %x_ref.1, bf16[2,1,8,3584]{3,2,1,0:T(8,128)(2,1)} %s_ref.3, bf16[1,8,3584]{2,1,0:T(8,128)(2,1)} %c_ref.1, bf16[1,3584]{1,0:T(2,128)(2,1)} %gain_ref.5, bf16[4,3584]{1,0:T(4,128)(2,1)} %bitcast.30, s32[2,1,2,8]{3,2,1,0:T(2,128)} %bitcast.34, ...), custom_call_target="tpu_custom_call" | custom-call | tf_op jit(solution)/shard_map/pallas_call | solution.py:387
  4.4 7.0 %all-to-all-start = ((bf16[16,24,3584]{2,1,0:T(8,128)(2,1)}), bf16[16,24,3584]{2,1,0:T(8,128)(2,1)S(1)}, u32[]{:S(2)}, u32[]{:S(2)}) async-start(bf16[16,24,3584]{2,1,0:T(8,128)(2,1)} %bitcast.46), calls=%async_computation | async-start | bytes 5505024 | tf_op jit(solution)/shard_map/all_to_all | solution.py:367
  11.4 1.9 %collective-permute-start.2 = (bf16[128,3584]{1,0:T(8,128)(2,1)}, bf16[128,3584]{1,0:T(8,128)(2,1)}, u32[]{:S(2)}, u32[]{:S(2)}) collective-permute-start(bf16[128,3584]{1,0:T(8,128)(2,1)} %bitcast.47), channel_id=1, source_target_pairs={{0,1},{1,0},{2,3},{3,2},{4,5},{5,4},{6,7},{7,6},{8,9},{9,8},{10,11... | collective-permute-start | bytes 2752520 | tf_op jit(solution)/shard_map/ppermute | solution.py:362
  13.4 2.3 %copy.15 = bf16[1,3584,128]{1,2,0:T(8,128)(2,1)} copy(bf16[1,3584,128]{2,1,0:T(8,128)(2,1)} %param.22) | data formatting | bytes 1835008 | tf_op args[10]
  15.7 2.4 %collective-permute-start.1 = (bf16[3584,128]{0,1:T(8,128)(2,1)}, bf16[3584,128]{0,1:T(8,128)(2,1)}, u32[]{:S(2)}, u32[]{:S(2)}) collective-permute-start(bf16[3584,128]{0,1:T(8,128)(2,1)} %bitcast.42), channel_id=1, source_target_pairs={{0,1},{1,0},{2,3},{3,2},{4,5},{5,4},{6,7},{7,6},{8,9},{9,8},{10,11... | collective-permute-start | bytes 2752520 | tf_op jit(solution)/shard_map/ppermute | solution.py:362
  18.1 2.3 %copy.14 = bf16[1,3584,128]{1,2,0:T(8,128)(2,1)} copy(bf16[1,3584,128]{2,1,0:T(8,128)(2,1)} %param.21) | data formatting | bytes 1835008 | tf_op args[9]
  20.3 0.0 copy-start.10
  20.3 0.0 copy-start.11
  20.3 2.0 %collective-permute-start = (bf16[3584,128]{0,1:T(8,128)(2,1)}, bf16[3584,128]{0,1:T(8,128)(2,1)S(1)}, u32[]{:S(2)}, u32[]{:S(2)}) collective-permute-start(bf16[3584,128]{0,1:T(8,128)(2,1)} %bitcast.44), channel_id=1, source_target_pairs={{0,1},{1,0},{2,3},{3,2},{4,5},{5,4},{6,7},{7,6},{8,9},{9,8},{10,11... | collective-permute-start | bytes 2752520 | tf_op jit(solution)/shard_map/ppermute | solution.py:362
  22.4 0.0 collective-permute-done.2
  22.4 2.8 %pad_maximum_fusion.1.down_hbm = bf16[256,3584]{1,0:T(8,128)(2,1)} fusion(bf16[128,3584]{1,0:T(8,128)(2,1)} %collective-permute-done.2, bf16[128,3584]{1,0:T(8,128)(2,1)} %bitcast.48), kind=kLoop, calls=%fused_computation.1 | loop fusion | flops 3670016 | bytes 3670016 | tf_op jit(solution)/shard_map/concatenate | solution.py:403
  25.2 0.0 collective-permute-done.1
  25.2 0.0 collective-permute-done
  25.2 0.0 copy-done.10
  25.2 0.0 copy-done.11
  25.2 3.0 %pad_maximum_fusion.gu_hbm = bf16[512,3584]{1,0:T(8,128)(2,1)} fusion(bf16[128,3584]{1,0:T(8,128)(2,1)} %bitcast.12, bf16[128,3584]{1,0:T(8,128)(2,1)S(1)} %bitcast.43, bf16[128,3584]{1,0:T(8,128)(2,1)S(1)} %bitcast.49, bf16[128,3584]{1,0:T(8,128)(2,1)S(1)} %bitcast.45), kind=kLoop, calls=%fused_computation | loop fusion | flops 14680064 | bytes 7340032 | tf_op jit(solution)/shard_map/concatenate | solution.py:402
  28.2 21.7 %all-to-all-done = bf16[16,24,3584]{2,1,0:T(8,128)(2,1)S(1)} async-done(((bf16[16,24,3584]{2,1,0:T(8,128)(2,1)}), bf16[16,24,3584]{2,1,0:T(8,128)(2,1)S(1)}, u32[]{:S(2)}, u32[]{:S(2)}) %all-to-all-start) | async-done | bytes 2752544 | tf_op jit(solution)/shard_map/all_to_all | solution.py:367
  50.0 0.0 copy-start
  50.0 0.0 copy-start.1
  50.0 0.0 copy-start.2
  50.0 0.0 copy-start.4
  50.0 0.0 copy-start.7
  50.0 0.0 copy-start.8
  50.0 0.0 copy-start.9
  50.0 9.1 %shard_map.132 = (bf16[8,2,24,1920]{3,2,1,0:T(8,128)(2,1)S(1)}, f32[192,512]{1,0:T(8,128)S(1)}) custom-call(bf16[384,3584]{1,0:T(8,128)(2,1)S(1)} %bitcast.23, bf16[512,3584]{1,0:T(8,128)(2,1)} %pad_maximum_fusion.gu_hbm, bf16[256,3584]{1,0:T(8,128)(2,1)} %pad_maximum_fusion.1.down_hbm), custom_call_target="tpu_custom_call" | custom-call | tf_op jit(solution)/shard_map/pallas_call | solution.py:351
  59.1 0.0 copy-start.5
  59.2 0.0 copy-start.6
  59.2 24.9 %all_to_all.44 = bf16[16,24,1920]{2,1,0:T(8,128)(2,1)S(1)} all-to-all(bf16[16,24,1920]{2,1,0:T(8,128)(2,1)S(1)} %bitcast.28), channel_id=1, replica_groups=mesh['pipe'=16,'x'=4,'y'=4,'core'=2] {'x','y'}, dimensions={0} | all-to-all | bytes 2949120 | tf_op jit(solution)/shard_map/all_to_all | solution.py:367
  84.1 0.0 copy-done
  84.1 0.0 copy-done.1
  84.1 0.0 copy-done.2
  84.1 0.0 copy-done.3
  84.1 0.0 copy-done.4
  84.1 0.0 copy-done.7
  84.2 0.0 copy-done.8
  84.2 0.0 copy-done.9
  84.2 1.0 shard_map.133
  85.2 5.0 %collective-permute-start.3 = (bf16[8,3584]{1,0:T(8,128)(2,1)S(1)}, bf16[8,3584]{1,0:T(8,128)(2,1)S(1)}, u32[]{:S(2)}, u32[]{:S(2)}) collective-permute-start(bf16[8,3584]{1,0:T(8,128)(2,1)S(1)} %get-tuple-element.15.y0_ref), channel_id=1, source_target_pairs={{0,32},{32,64},{64,96},{96,128},{128,160},{160,192},{192,224},{224... | collective-permute-start | bytes 172040 | tf_op jit(solution)/shard_map/ppermute | solution.py:373
  90.2 1.9 %collective-permute-start.4 = (bf16[8,3584]{1,0:T(8,128)(2,1)S(1)}, bf16[8,3584]{1,0:T(8,128)(2,1)S(1)}, u32[]{:S(2)}, u32[]{:S(2)}) collective-permute-start(bf16[8,3584]{1,0:T(8,128)(2,1)S(1)} %get-tuple-element.16.b0_ref), channel_id=1, source_target_pairs={{32,0},{64,32},{96,64},{128,96},{160,128},{192,160},{224,192},{256... | collective-permute-start | bytes 172040 | tf_op jit(solution)/shard_map/ppermute | solution.py:373
  92.1 0.0 collective-permute-done.3.y_ref
  92.2 5.3 %collective-permute-done.4.b_ref = bf16[8,3584]{1,0:T(8,128)(2,1)S(1)} collective-permute-done((bf16[8,3584]{1,0:T(8,128)(2,1)S(1)}, bf16[8,3584]{1,0:T(8,128)(2,1)S(1)}, u32[]{:S(2)}, u32[]{:S(2)}) %collective-permute-start.4) | collective-permute-done | bytes 57376 | tf_op jit(solution)/shard_map/ppermute | solution.py:373
  97.5 0.0 copy-done.5
  97.5 0.0 copy-done.6
  97.5 0.7 shard_map.134
  98.2 19.9 %all_to_all.45 = bf16[16,24,1792]{2,1,0:T(8,128)(2,1)S(1)} all-to-all(bf16[16,24,1792]{2,1,0:T(8,128)(2,1)S(1)} %bitcast.29), channel_id=1, replica_groups=mesh['pipe'=16,'x'=4,'y'=4,'core'=2] {'x','y'}, dimensions={0} | all-to-all | bytes 2752512 | tf_op jit(solution)/shard_map/all_to_all | solution.py:367
  118.2 6.1 %shard_map.135 = bf16[8,2,24,1920]{3,2,1,0:T(8,128)(2,1)S(1)} custom-call(bf16[384,1792]{1,0:T(8,128)(2,1)S(1)} %bitcast.27, f32[192,512]{1,0:T(8,128)S(1)} %get-tuple-element.18.keep_ref, bf16[512,3584]{1,0:T(8,128)(2,1)} %pad_maximum_fusion.gu_hbm, bf16[256,3584]{1,0:T(8,128)(2,1)} %pad_maximum_fusion.1.down_hbm), custom_call_target="tpu_custom_call" | custom-call | tf_op jit(solution)/shard_map/pallas_call | solution.py:351
  124.3 19.6 %all_to_all.46 = bf16[16,24,1920]{2,1,0:T(8,128)(2,1)S(1)} all-to-all(bf16[16,24,1920]{2,1,0:T(8,128)(2,1)S(1)} %bitcast.26), channel_id=1, replica_groups=mesh['pipe'=16,'x'=4,'y'=4,'core'=2] {'x','y'}, dimensions={0} | all-to-all | bytes 2949120 | tf_op jit(solution)/shard_map/all_to_all | solution.py:367
  143.9 1.6 %shard_map.136 = (bf16[2,1,8,3584]{3,2,1,0:T(8,128)(2,1)}, bf16[2,1,8,3584]{3,2,1,0:T(8,128)(2,1)}) custom-call(bf16[384,1920]{1,0:T(8,128)(2,1)S(1)} %bitcast.24, bf16[8,3584]{1,0:T(8,128)(2,1)S(1)} %get-tuple-element.19.x_ref, bf16[2,1,8,3584]{3,2,1,0:T(8,128)(2,1)S(1)} %copy-done, bf16[8,3584]{1,0:T(8,128)(2,1)S(1)} %get-tuple-element.20.c_ref, ...), custom_call_target="tpu_custom_call" | custom-call | tf_op jit(solution)/shard_map/pallas_call | solution.py:351
  (1 shorter events, 0.0 us)
Async XLA Ops:
  4.4 45.6 %all-to-all-start = ((bf16[16,24,3584]{2,1,0:T(8,128)(2,1)}), bf16[16,24,3584]{2,1,0:T(8,128)(2,1)S(1)}, u32[]{:S(2)}, u32[]{:S(2)}) async-start(bf16[16,24,3584]{2,1,0:T(8,128)(2,1)} %bitcast.46), calls=%async_computation | async-start | bytes 5505024 | tf_op jit(solution)/shard_map/all_to_all | solution.py:367
  11.4 10.9 %collective-permute-start.2 = (bf16[128,3584]{1,0:T(8,128)(2,1)}, bf16[128,3584]{1,0:T(8,128)(2,1)}, u32[]{:S(2)}, u32[]{:S(2)}) collective-permute-start(bf16[128,3584]{1,0:T(8,128)(2,1)} %bitcast.47), channel_id=1, source_target_pairs={{0,1},{1,0},{2,3},{3,2},{4,5},{5,4},{6,7},{7,6},{8,9},{9,8},{10,11... | collective-permute-start | bytes 2752520 | tf_op jit(solution)/shard_map/ppermute | solution.py:362
  15.7 9.6 %collective-permute-start.1 = (bf16[3584,128]{0,1:T(8,128)(2,1)}, bf16[3584,128]{0,1:T(8,128)(2,1)}, u32[]{:S(2)}, u32[]{:S(2)}) collective-permute-start(bf16[3584,128]{0,1:T(8,128)(2,1)} %bitcast.42), channel_id=1, source_target_pairs={{0,1},{1,0},{2,3},{3,2},{4,5},{5,4},{6,7},{7,6},{8,9},{9,8},{10,11... | collective-permute-start | bytes 2752520 | tf_op jit(solution)/shard_map/ppermute | solution.py:362
  20.3 4.9 %copy-start.10 = (bf16[1,3584,128]{1,2,0:T(8,128)(2,1)S(1)}, bf16[1,3584,128]{1,2,0:T(8,128)(2,1)}, u32[]{:S(2)}) copy-start(bf16[1,3584,128]{1,2,0:T(8,128)(2,1)} %copy.15) | copy-start | bytes 2752516
  20.3 4.9 %copy-start.11 = (bf16[1,3584,128]{1,2,0:T(8,128)(2,1)S(1)}, bf16[1,3584,128]{1,2,0:T(8,128)(2,1)}, u32[]{:S(2)}) copy-start(bf16[1,3584,128]{1,2,0:T(8,128)(2,1)} %copy.14) | copy-start | bytes 2752516
  20.3 4.9 %collective-permute-start = (bf16[3584,128]{0,1:T(8,128)(2,1)}, bf16[3584,128]{0,1:T(8,128)(2,1)S(1)}, u32[]{:S(2)}, u32[]{:S(2)}) collective-permute-start(bf16[3584,128]{0,1:T(8,128)(2,1)} %bitcast.44), channel_id=1, source_target_pairs={{0,1},{1,0},{2,3},{3,2},{4,5},{5,4},{6,7},{7,6},{8,9},{9,8},{10,11... | collective-permute-start | bytes 2752520 | tf_op jit(solution)/shard_map/ppermute | solution.py:362
  50.0 34.2 %copy-start = (bf16[2,1,8,3584]{3,2,1,0:T(8,128)(2,1)S(1)}, bf16[2,1,8,3584]{3,2,1,0:T(8,128)(2,1)}, u32[]{:S(2)}) copy-start(bf16[2,1,8,3584]{3,2,1,0:T(8,128)(2,1)} %s_ref.3) | copy-start | bytes 344068
  50.0 34.2 %copy-start.1 = (bf16[1,3584,4]{1,2,0:T(4,128)(2,1)S(1)}, bf16[1,3584,4]{1,2,0:T(4,128)(2,1)}, u32[]{:S(2)}) copy-start(bf16[1,3584,4]{1,2,0:T(4,128)(2,1)} %param.20) | copy-start | bytes 86020
  50.0 34.2 %copy-start.2 = (bf16[1,8,3584]{2,1,0:T(8,128)(2,1)S(1)}, bf16[1,8,3584]{2,1,0:T(8,128)(2,1)}, u32[]{:S(2)}) copy-start(bf16[1,8,3584]{2,1,0:T(8,128)(2,1)} %x_ref.1) | copy-start | bytes 172036
  50.0 34.2 %copy-start.3 = (bf16[1,8,3584]{2,1,0:T(8,128)(2,1)S(1)}, bf16[1,8,3584]{2,1,0:T(8,128)(2,1)}, u32[]{:S(2)}) copy-start(bf16[1,8,3584]{2,1,0:T(8,128)(2,1)} %c_ref.1) | copy-start | bytes 172036
  50.0 34.2 %copy-start.4 = (bf16[1,3584]{1,0:T(2,128)(2,1)S(1)}, bf16[1,3584]{1,0:T(2,128)(2,1)}, u32[]{:S(2)}) copy-start(bf16[1,3584]{1,0:T(2,128)(2,1)} %gain_ref.5) | copy-start | bytes 21508
  50.0 34.2 %copy-start.7 = (f32[3,8,128]{2,1,0:T(8,128)S(1)}, f32[3,8,128]{2,1,0:T(8,128)}, u32[]{:S(2)}) copy-start(f32[3,8,128]{2,1,0:T(8,128)} %get-tuple-element.14.stat_ref) | copy-start | bytes 36868
  50.0 34.2 %copy-start.8 = (s32[2,1,8,2]{2,3,1,0:T(2,128)S(1)}, s32[2,1,8,2]{2,3,1,0:T(2,128)}, u32[]{:S(2)}) copy-start(s32[2,1,8,2]{2,3,1,0:T(2,128)} %param.17) | copy-start | bytes 388
  50.0 34.2 %copy-start.9 = (s32[2,1,8,2]{2,3,1,0:T(2,128)S(1)}, s32[2,1,8,2]{2,3,1,0:T(2,128)}, u32[]{:S(2)}) copy-start(s32[2,1,8,2]{2,3,1,0:T(2,128)} %param.18) | copy-start | bytes 388
  59.1 38.4 %copy-start.5 = (bf16[1,8,3584]{2,1,0:T(8,128)(2,1)S(1)}, bf16[1,8,3584]{2,1,0:T(8,128)(2,1)}, u32[]{:S(2)}) copy-start(bf16[1,8,3584]{2,1,0:T(8,128)(2,1)} %fnew_ref.1) | copy-start | bytes 172036
  59.2 38.3 %copy-start.6 = (bf16[1,8,3584]{2,1,0:T(8,128)(2,1)S(1)}, bf16[1,8,3584]{2,1,0:T(8,128)(2,1)}, u32[]{:S(2)}) copy-start(bf16[1,8,3584]{2,1,0:T(8,128)(2,1)} %gnew_ref.1) | copy-start | bytes 172036
  85.2 7.0 %collective-permute-start.3 = (bf16[8,3584]{1,0:T(8,128)(2,1)S(1)}, bf16[8,3584]{1,0:T(8,128)(2,1)S(1)}, u32[]{:S(2)}, u32[]{:S(2)}) collective-permute-start(bf16[8,3584]{1,0:T(8,128)(2,1)S(1)} %get-tuple-element.15.y0_ref), channel_id=1, source_target_pairs={{0,32},{32,64},{64,96},{96,128},{128,160},{160,192},{192,224},{224... | collective-permute-start | bytes 172040 | tf_op jit(solution)/shard_map/ppermute | solution.py:373
  90.2 7.3 %collective-permute-start.4 = (bf16[8,3584]{1,0:T(8,128)(2,1)S(1)}, bf16[8,3584]{1,0:T(8,128)(2,1)S(1)}, u32[]{:S(2)}, u32[]{:S(2)}) collective-permute-start(bf16[8,3584]{1,0:T(8,128)(2,1)S(1)} %get-tuple-element.16.b0_ref), channel_id=1, source_target_pairs={{32,0},{64,32},{96,64},{128,96},{160,128},{192,160},{224,192},{256... | collective-permute-start | bytes 172040 | tf_op jit(solution)/shard_map/ppermute | solution.py:373
